TPU v7x, 32 devices: a whole 2x2x4 slice. The times are simulated.
32 devices in a mesh: wide: 8 (over z, y), narrow: 4 (over x, core).
Axes of the slice: x: 2, y: 2, z: 4, core: 2. Of those that a mesh axis runs over, the one named last changes fastest.
Arguments:
- factors: bfloat16 [15, 7168, 1920], P(None, ('wide', 'narrow')), may hold values from -0.625 to 0.625
- t2_window: bfloat16 [16, 15, 15], replicated, may hold values from -0.3984375 to 0.3984375
- residual_in: bfloat16 [232, 16, 16384], P('wide', 'narrow'), may hold values from -6 to 6
- tile_mask: int32 [225], replicated, may hold values from 0 to 1, as said below
- owner_slot: int32 [225], replicated, may hold values from 0 to 15, as said below
- home_slot: int32 [225], replicated, may hold values from 0 to 231, as said below
Outputs:
- residual_out: bfloat16 [232, 16, 16384], P('wide', 'narrow')
- ladder_norms: float32 [16, 16], P('wide', 'narrow')
Inputs may be any that keep to these rules, and one draw needn't show every extreme that they name: `tile_mask`: exactly 16 tiles are filled. `owner_slot`: the filled tiles take the owner slots 0 to 15, one each; slot o belongs to wide index o // 2; the filled tiles of one wide index have different home wide indices. Entries of tiles that are not filled mean nothing. `home_slot`: all different; home slot s lies on wide index s // 29.
All inputs are finite; a program needn't handle non-finite values.
Results may differ from a plain program's by a relative error of at most 0.0045.
Values may be sent and summed in bfloat16 or wider, within the bound.
No kernel may reach another device: no remote copies, remote signals or barrier semaphores. Data moves between devices by JAX's collectives and lax.ppermute only.
A program may use at most 192 MiB of HBM per device.

v0:
```python
import jax
import jax.numpy as jnp
from jax import lax
from jax.sharding import PartitionSpec as P

SLOTS = 2


def tile_contract(first_side, second_side, amplitude, window):
    precise = lax.Precision.HIGHEST
    tile_width = first_side.shape[1] // window
    integral = lax.dot_general(
        first_side, second_side, (((0,), (0,)), ((), ())), preferred_element_type=jnp.float32
    )
    accumulated = jnp.einsum(
        "cadb,pcd->pab",
        integral.reshape(window, tile_width, window, tile_width),
        amplitude,
        precision=precise,
    )
    return accumulated.reshape(amplitude.shape[0], tile_width * tile_width)


def body(factors, t2_window, residual_in, tile_mask, owner_slot, home_slot):
    owner_count = lax.axis_size("wide")
    clusters = factors.shape[0]
    window = t2_window.shape[1]
    amplitude = t2_window.astype(jnp.float32)
    filled_total = owner_count * SLOTS
    tile_ids = jnp.arange(tile_mask.shape[0], dtype=jnp.int32)
    is_filled = tile_mask == 1
    owner_match = is_filled[:, None] & (
        owner_slot[:, None] == jnp.arange(filled_total, dtype=jnp.int32)[None, :]
    )
    tile_of_slot = jnp.sum(jnp.where(owner_match, tile_ids[:, None], 0), axis=0)
    slot_pairs = tile_of_slot.reshape(owner_count, SLOTS)
    cluster_ids = jnp.stack([slot_pairs // clusters, slot_pairs % clusters], axis=2)
    outgoing = jnp.take(factors, cluster_ids, axis=0)
    received = lax.all_to_all(outgoing, "wide", split_axis=0, concat_axis=0, tiled=True)
    aux_rows = received.shape[0] * received.shape[3]

    def one_tile(position):
        slot_blocks = lax.dynamic_index_in_dim(received, position, 1, keepdims=False)
        first_side = slot_blocks[:, 0].reshape(aux_rows, slot_blocks.shape[-1])
        second_side = slot_blocks[:, 1].reshape(aux_rows, slot_blocks.shape[-1])
        return tile_contract(first_side, second_side, amplitude, window)

    partial_terms = lax.map(one_tile, jnp.arange(received.shape[1], dtype=jnp.int32))
    ladder = lax.psum_scatter(partial_terms, "narrow", scatter_dimension=1, tiled=True).astype(
        jnp.bfloat16
    )
    ladder_wide = ladder.astype(jnp.float32)
    ladder_norms = jnp.mean(ladder_wide * ladder_wide, axis=2)
    home_count = residual_in.shape[0]
    home_ids = lax.axis_index("wide") * home_count + jnp.arange(home_count, dtype=jnp.int32)
    present = is_filled[:, None] & (home_slot[:, None] == home_ids[None, :])
    kept_slot = jnp.any(present, axis=0)
    source_slot = jnp.sum(jnp.where(present, owner_slot[:, None], 0), axis=0)
    gathered_rows = lax.all_gather(ladder, "wide", axis=0, tiled=True)
    owner_rows = jnp.arange(gathered_rows.shape[0], dtype=jnp.int32)
    pick_matrix = (source_slot[:, None] == owner_rows[None, :]) & kept_slot[:, None]
    home_ladder = jnp.einsum(
        "jm,mpx->jpx",
        pick_matrix.astype(jnp.bfloat16),
        gathered_rows,
        preferred_element_type=jnp.float32,
    )
    combined = residual_in.astype(jnp.float32) + home_ladder
    residual_out = jnp.where(kept_slot[:, None, None], combined, 0.0).astype(jnp.bfloat16)
    return (residual_out, ladder_norms)


def solution(mesh):
    in_specs = (P(None, ("wide", "narrow"), None), P(), P("wide", "narrow", None), P(), P(), P())
    out_specs = (P("wide", "narrow", None), P("wide", "narrow"))
    return jax.shard_map(body, mesh=mesh, in_specs=in_specs, out_specs=out_specs, check_vma=False)
```

profile of v0, /device:TPU:0, one launch (start us, length us, event | category | flops | bytes accessed | tf_op | source)
XLA Modules:
  0.0 962.8 jit_solution(7567127638257354576)
XLA Ops:
  9.6 15.9 %gather_fusion = bf16[32,224,1920]{2,1,0:T(8,128)(2,1)} fusion(bf16[15,224,1920]{2,1,0:T(8,128)(2,1)} %param.8, s32[1024]{0:T(1024)S(1)} %pad_clamp_fusion), kind=kCustom, calls=%fused_computation | custom fusion | bytes 55050368 | tf_op jit(solution)/shard_map/jit(_take)/gather | solution.py:38
  25.5 19.1 %broadcast_select_fusion = bf16[8,2,2,224,1920]{4,3,2,1,0:T(8,128)(2,1)} fusion(bf16[8,2,2,224,1920]{4,3,2,1,0:T(8,128)(2,1)} %bitcast.63, pred[8,2,2]{2,1,0:T(4,128)(4,1)S(1)} %copy.59), kind=kLoop, calls=%fused_computation.7 | loop fusion | flops 13762560 | bytes 55050272 | tf_op jit(solution)/shard_map/jit(_take)/select_n | solution.py:38
  44.6 7.4 all-to-all-start
  53.4 593.4 %all-to-all-done = bf16[8,2,2,224,1920]{4,3,2,1,0:T(8,128)(2,1)} async-done(((bf16[8,2,2,224,1920]{4,3,2,1,0:T(8,128)(2,1)}), bf16[8,2,2,224,1920]{4,3,2,1,0:T(8,128)(2,1)}, u32[]{:S(2)}, u32[]{:S(2)}) %all-to-all-start) | async-done | bytes 27525152 | tf_op jit(solution)/shard_map/all_to_all | solution.py:39
  646.8 204.0 %while.10 = (s32[]{:T(128)}, f32[2,16,16384]{2,0,1:T(2,128)S(1)}, s32[2]{0:T(128)S(1)}, bf16[8,2,2,224,1920]{4,3,2,1,0:T(8,128)(2,1)}, f32[16,15,15]{2,0,1:T(8,128)S(1)}, /*index=5*/s32[]{:T(128)}, s32[]{:T(128)}, s32[]{:T(128)}) while((s32[]{:T(128)}, f32[2,16,16384]{2,0,1:T(2,128)S(1)}, s32[2]{0:T(128)S(1)}, ...), condition=%wide.region_4.5_spmd, body=%wide.region_3.4_spmd.sunk | while | flops 13919846400 | bytes 131086536 | solution.py:48
  666.0 7.2 copy_bitcast_fusion.2
  673.3 5.4 fusion.31
  678.6 9.9 %copy.90 = bf16[1920,1792]{1,0:T(8,128)(2,1)} copy(bf16[1920,1792]{0,1:T(8,128)(2,1)} %bitcast.60) | data formatting | bytes 13762560 | tf_op jit(solution)/shard_map/while/body/eval_jaxpr/dot_general | solution.py:12
  688.6 9.8 %copy.91 = bf16[1920,1792]{1,0:T(8,128)(2,1)} copy(bf16[1920,1792]{0,1:T(8,128)(2,1)} %bitcast.59) | data formatting | bytes 13762560 | tf_op jit(solution)/shard_map/while/body/eval_jaxpr/dot_general | solution.py:12
  698.3 20.6 %fusion.32 = f32[15,128,15,128]{3,1,2,0:T(8,128)S(1)} fusion(bf16[15,128,1792,1]{2,1,3,0:T(8,128)(2,1)} %bitcast.61, bf16[15,128,1792,1]{2,1,0,3:T(8,128)(2,1)} %bitcast.62), kind=kOutput, calls=%fused_computation.39.clone.1 | convolution fusion | flops 13212057600 | bytes 28508160 | tf_op jit(solution)/shard_map/while/body/eval_jaxpr/dot_general | solution.py:12
  718.9 20.3 %fusion.33 = f32[16,128,128]{2,0,1:T(8,128)S(1)} fusion(f32[15,128,15,128]{3,1,2,0:T(8,128)S(1)} %fusion.32, f32[16,15,15]{2,0,1:T(8,128)S(1)} %get-tuple-element.128), kind=kOutput, calls=%fused_computation.4.clone.1 | convolution fusion | flops 707788800 | bytes 15808576 | tf_op jit(solution)/shard_map/while/body/eval_jaxpr/cadb,pcd->pab/dot_general | solution.py:15
  739.6 13.2 %dynamic_update_slice.5 = f32[2,16,16384]{2,0,1:T(2,128)S(1)} dynamic-update-slice(f32[2,16,16384]{2,0,1:T(2,128)S(1)} %get-tuple-element.117, f32[1,16,16384]{2,0,1:T(1,128)S(1)} %bitcast.64, s32[]{:T(128)} %get-tuple-element.116, s32[]{:T(128)} %constant.57.clone.1..sunk, s32[]{:T(128)} %constant.57.clone.1..sunk) | dynamic-update-slice | bytes 2097156 | tf_op jit(solution)/shard_map/while/body/jit(dynamic_update_index_in_dim)/dynamic_update_slice | solution.py:48
  755.3 7.2 copy_bitcast_fusion.2
  762.5 5.4 fusion.31
  767.9 9.9 %copy.90 = bf16[1920,1792]{1,0:T(8,128)(2,1)} copy(bf16[1920,1792]{0,1:T(8,128)(2,1)} %bitcast.60) | data formatting | bytes 13762560 | tf_op jit(solution)/shard_map/while/body/eval_jaxpr/dot_general | solution.py:12
  777.9 9.8 %copy.91 = bf16[1920,1792]{1,0:T(8,128)(2,1)} copy(bf16[1920,1792]{0,1:T(8,128)(2,1)} %bitcast.59) | data formatting | bytes 13762560 | tf_op jit(solution)/shard_map/while/body/eval_jaxpr/dot_general | solution.py:12
  787.6 20.6 %fusion.32 = f32[15,128,15,128]{3,1,2,0:T(8,128)S(1)} fusion(bf16[15,128,1792,1]{2,1,3,0:T(8,128)(2,1)} %bitcast.61, bf16[15,128,1792,1]{2,1,0,3:T(8,128)(2,1)} %bitcast.62), kind=kOutput, calls=%fused_computation.39.clone.1 | convolution fusion | flops 13212057600 | bytes 28508160 | tf_op jit(solution)/shard_map/while/body/eval_jaxpr/dot_general | solution.py:12
  808.2 20.3 %fusion.33 = f32[16,128,128]{2,0,1:T(8,128)S(1)} fusion(f32[15,128,15,128]{3,1,2,0:T(8,128)S(1)} %fusion.32, f32[16,15,15]{2,0,1:T(8,128)S(1)} %get-tuple-element.128), kind=kOutput, calls=%fused_computation.4.clone.1 | convolution fusion | flops 707788800 | bytes 15808576 | tf_op jit(solution)/shard_map/while/body/eval_jaxpr/cadb,pcd->pab/dot_general | solution.py:15
  828.9 13.2 %dynamic_update_slice.5 = f32[2,16,16384]{2,0,1:T(2,128)S(1)} dynamic-update-slice(f32[2,16,16384]{2,0,1:T(2,128)S(1)} %get-tuple-element.117, f32[1,16,16384]{2,0,1:T(1,128)S(1)} %bitcast.64, s32[]{:T(128)} %get-tuple-element.116, s32[]{:T(128)} %constant.57.clone.1..sunk, s32[]{:T(128)} %constant.57.clone.1..sunk) | dynamic-update-slice | bytes 2097156 | tf_op jit(solution)/shard_map/while/body/jit(dynamic_update_index_in_dim)/dynamic_update_slice | solution.py:48
  850.7 40.1 %all-reduce.2 = bf16[2,16,16384]{2,0,1:T(2,128)(2,1)S(1)} all-reduce(f32[2,16,16384]{2,0,1:T(2,128)S(1)} %get-tuple-element.29), channel_id=2, replica_groups=mesh['wide'=8,'narrow'=4] {'narrow'}, use_global_device_ids=true, to_apply=%region_5.6.clone | all-reduce | flops 524288 | bytes 3145728
  891.4 0.9 copy.65
  893.4 47.3 %all-gather.2.cloned.1.call-done = bf16[16,4,16384]{2,1,0:T(4,128)(2,1)} async-done(((bf16[2,4,16384]{2,1,0:T(4,128)(2,1)}), bf16[16,4,16384]{2,1,0:T(4,128)(2,1)}) %all-gather.2.cloned.1.call-update) | async-done | bytes 2097168 | tf_op jit(solution)/shard_map/all_gather | solution.py:59
  940.7 10.2 %fusion.7 = bf16[29,4,16384]{2,0,1:T(8,128)(2,1)S(1)} fusion(bf16[29,4,16384]{2,1,0:T(4,128)(2,1)} %param.10, pred[29]{0:T(512)(128)(4,1)S(1)} %fusion.9, bf16[16,4,16384]{2,1,0:T(4,128)(2,1)} %all-gather.2.cloned.1.call-done, s32[29]{0:T(128)S(1)} %select_reduce_fusion), kind=kOutput, calls=%fused_computation.10 | convolution fusion | flops 68420512 | bytes 9699473 | tf_op jit(solution)/shard_map/jm,mpx->jpx/dot_general | solution.py:62
  950.9 4.9 copy.67
  (46 shorter events, 6.6 us)
Async XLA Ops:
  7.8 0.8 copy-start.1
  44.6 7.5 copy-start
  44.6 7.5 copy-start.5
  44.6 602.1 %all-to-all-start = ((bf16[8,2,2,224,1920]{4,3,2,1,0:T(8,128)(2,1)}), bf16[8,2,2,224,1920]{4,3,2,1,0:T(8,128)(2,1)}, u32[]{:S(2)}, u32[]{:S(2)}) async-start(bf16[8,2,2,224,1920]{4,3,2,1,0:T(8,128)(2,1)} %broadcast_select_fusion), calls=%async_computation | async-start | bytes 55050240 | tf_op jit(solution)/shard_map/all_to_all | solution.py:39
  52.1 888.6 %all-gather.2.cloned.1.call-start = ((), (), s32[]{:S(2)}) async-start(), calls=%async_computation.1 | async-start | bytes 2359296 | tf_op jit(solution)/shard_map/all_gather | solution.py:59
  646.8 245.6 %copy-start.2 = (pred[225]{0:T(512)(128)(4,1)S(1)}, pred[225]{0:T(512)(128)(4,1)}, u32[]{:S(2)}) copy-start(pred[225]{0:T(512)(128)(4,1)} %copy-done.1) | copy-start | bytes 679
  646.8 245.6 %copy-start.3 = (s32[225]{0:T(256)S(1)}, s32[225]{0:T(256)}, u32[]{:S(2)}) copy-start(s32[225]{0:T(256)} %param.13) | copy-start | bytes 2704
  646.8 245.8 %copy-start.4 = (s32[225]{0:T(256)S(1)}, s32[225]{0:T(256)}, u32[]{:S(2)}) copy-start(s32[225]{0:T(256)} %param.12) | copy-start | bytes 2704
Sparse Core Ops, SparseCore 0:
  892.4 48.2 all-gather.1
where the time goes:
time: 966 us; the launch traced here: 963 us
  waiting for transfers between devices  641 us (66%)
  local copies, waits for them, and re-layouts  117 us (12%)
  matrix products  92 us (10%)
  blocking collectives  40.1 us (4%)
  loops' own time  29.2 us (3%)
  other arithmetic  21.5 us (2%)
  between operations  15 us (2%)
    all_to_all x1, waiting for transfers between devices, body(): lax.all_to_all(outgoing, 'wide', split_axis=0, concat_axis=0, tiled=True)  593 us
    all_gather x1, waiting for transfers between devices, body(): gathered_rows = lax.all_gather(ladder, 'wide', axis=0, tiled=True)  47.3 us
    dot_general x2, matrix products, tile_contract(): lax.dot_general(first_side, second_side, (((0,), (0,)), ((), ())), prefer...  41.2 us
    dot_general x2, matrix products, tile_contract(): jnp.einsum('cadb,pcd->pab', integral.reshape(window, tile_width, window,...  40.7 us
    unnamed x1, blocking collectives  40.1 us
    dot_general x4, local copies, waits for them, and re-layouts, tile_contract(): lax.dot_general(first_side, second_side, (((0,), (0,)), ((), ())), prefer...  39.4 us
    another operation x1, loops' own time, body(): lax.map(one_tile, jnp.arange(received.shape[1], dtype=jnp.int32))  29.2 us
    dynamic_update_slice x2, local copies, waits for them, and re-layouts, body(): lax.map(one_tile, jnp.arange(received.shape[1], dtype=jnp.int32))  26.4 us
  transfers between devices with their start and end apart: 2, of which 2 were waited for; matrix products, arithmetic and copies ran while one was open for 0% of the time, Pallas kernels for 0%

commit v1 on v0

v1 whole, which is shorter than its diff:
```python
import functools

import jax
import jax.numpy as jnp
from jax import lax
from jax.experimental import pallas as pl
from jax.experimental.pallas import tpu as pltpu
from jax.sharding import PartitionSpec as P

SLOTS = 2
ROWS = 16
WIDTH = 128
DEPTH = 256
TOGETHER = 4
STEP = 3
LADDER_VMEM = 52 * 1024 * 1024
SMALL_VMEM = 24 * 1024 * 1024
GATHER_VMEM = 60 * 1024 * 1024
HBM = pl.BlockSpec(memory_space=pltpu.HBM)


class Layout:
    def __init__(self, owners, homes):
        sizes = dict(
            own_first=owners,
            own_second=owners,
            partner_first=owners,
            partner_second=owners,
            pick=owners,
            arrive=owners + 1,
            filled=homes,
            norm=SLOTS,
            matched=1,
            half=1,
        )
        self.size = 0
        for name, size in sizes.items():
            setattr(self, name, self.size)
            self.size += size


def plan_kernel(
    place, table, plan, tile_of, home_of, official, wide_of, spot, room, load, used, slot_tile, slot_home, good,
    *, layout, names, clusters, homes
):
    wide, half = place[0], place[1]
    owners = len(names)
    filled = owners * SLOTS
    across = owners // 2

    def each(count, step, unroll=1):
        def run(i, carry):
            step(i)
            return carry

        lax.fori_loop(0, count, run, 0, unroll=unroll)

    def list_tile(t, count):
        entry = table[t]
        tile_of[count] = t
        home_of[count] = entry
        return count + (entry & 1)

    total = table.shape[0]
    lax.fori_loop(0, total, list_tile, 0, unroll=5 if total % 5 == 0 else 1)

    def clear_wide(w):
        room[w] = SLOTS
        load[w] = 0

    def clear_used(i):
        used[i] = 0

    each(owners, clear_wide)
    each(owners * owners, clear_used, 8)

    def count_home(i):
        entry = home_of[i] // SLOTS
        official[i] = entry % filled
        home_of[i] = entry // filled
        wide_of[i] = home_of[i] // homes
        load[wide_of[i]] = load[wide_of[i]] + 1
        spot[i] = -1

    each(filled, count_home)
    good[0] = 1

    def put(i, w):
        spot[i] = w * SLOTS + SLOTS - room[w]
        room[w] = room[w] - 1

    low = lax.fori_loop(0, across, lambda h, x: x + load[h], 0)
    excess = jnp.abs(low - owners)
    begin = jnp.where(low > owners, 0, across)

    def move_one(r):
        @pl.when(r < excess)
        def _():
            def fuller(h, best):
                better = (load[begin + h] > best[1]) & (used[((begin + h) ^ across) * owners + begin + h] == 0)
                return jnp.where(better, begin + h, best[0]), jnp.where(better, load[begin + h], best[1])

            best, most = lax.fori_loop(0, across, fuller, (jnp.int32(0), jnp.int32(0)))

            @pl.when(most == 0)
            def _():
                good[0] = 0

            @pl.when(most > 0)
            def _():
                found = lax.fori_loop(
                    0, filled, lambda i, x: jnp.where((wide_of[i] == best) & (spot[i] < 0), i, x), jnp.int32(0)
                )
                put(found, best ^ across)
                used[(best ^ across) * owners + best] = 1
                load[best] = load[best] - 1

    @pl.when(excess > across)
    def _():
        good[0] = 0

    each(across, move_one)

    def put_home(i):
        @pl.when((spot[i] < 0) & (room[wide_of[i]] > 0))
        def _():
            put(i, wide_of[i])

    each(filled, put_home)

    def put_near(i):
        @pl.when(spot[i] < 0)
        def _():
            def try_near(k):
                w = wide_of[i] ^ (k + 1)

                @pl.when((spot[i] < 0) & (room[w] > 0) & (used[w * owners + wide_of[i]] == 0))
                def _():
                    put(i, w)
                    used[w * owners + wide_of[i]] = 1

            each(across - 1, try_near)

            @pl.when(spot[i] < 0)
            def _():
                good[0] = 0

    each(filled, put_near)

    @pl.when(good[0] == 0)
    def _():
        def keep_owner(i):
            spot[i] = official[i]

        each(filled, keep_owner)

    def clear_filled(i):
        plan[layout.filled + i] = 0

    each(homes, clear_filled)

    def enter(i):
        slot_tile[spot[i]] = tile_of[i]
        slot_home[spot[i]] = home_of[i]

        @pl.when(official[i] // SLOTS == wide)
        def _():
            plan[layout.norm + official[i] % SLOTS] = ((spot[i] // SLOTS) ^ wide) * SLOTS + spot[i] % SLOTS

        @pl.when(wide_of[i] == wide)
        def _():
            plan[layout.filled + home_of[i] - wide * homes] = 1

    each(filled, enter)

    for j, name in enumerate(names):
        base = (wide ^ name) * SLOTS
        own, other = slot_tile[base + half], slot_tile[base + 1 - half]
        plan[layout.own_first + j] = own // clusters
        plan[layout.own_second + j] = own % clusters
        plan[layout.partner_first + j] = other // clusters
        plan[layout.partner_second + j] = other % clusters

    def at_home(slot, w):
        local = slot_home[slot] - w * homes
        return jnp.where((local >= 0) & (local < homes), local, -1)

    mine = wide * SLOTS
    plan[layout.arrive] = at_home(mine + half, wide)
    plan[layout.arrive + 1] = at_home(mine + 1 - half, wide)

    def meet(k):
        w = wide ^ k
        plan[layout.arrive + 1 + k] = jnp.maximum(at_home(w * SLOTS, wide), at_home(w * SLOTS + 1, wide))
        second = (at_home(mine + 1, w) >= 0).astype(jnp.int32)
        plan[layout.pick + k] = second ^ half

    def meet_later(k):
        meet(k + 1)

    plan[layout.pick] = 0
    each(owners - 1, meet_later)
    plan[layout.matched] = good[0]
    plan[layout.half] = half


def make_plan(place, tile_mask, owner_slot, home_slot, layout, names, clusters, homes):
    owners = len(names)
    filled = owners * SLOTS
    smem = pl.BlockSpec(memory_space=pltpu.SMEM)
    lists = [filled + 1] * 3 + [filled] * 2 + [owners] * 2 + [owners * owners] + [filled] * 2 + [1]
    return pl.pallas_call(
        functools.partial(plan_kernel, layout=layout, names=names, clusters=clusters, homes=homes),
        in_specs=[smem] * 2,
        out_specs=smem,
        out_shape=jax.ShapeDtypeStruct((layout.size,), jnp.int32),
        scratch_shapes=[pltpu.SMEM((size,), jnp.int32) for size in lists],
        compiler_params=pltpu.CompilerParams(vmem_limit_bytes=SMALL_VMEM),
    )(place, tile_mask + SLOTS * (owner_slot + filled * home_slot))


def turn_columns(source, target, slot, d, place):
    columns = pl.ds(pl.multiple_of(d * WIDTH, WIDTH), WIDTH)
    rows = source.shape[-2]
    view = source.at[0, 0] if len(source.shape) == 4 else source.at[0]
    target[slot, columns, place : place + rows] = view[:, columns].T


def partial_kernel(plan, *refs, layout, window, rows, is_first, is_last, waits, gathers):
    refs = list(refs)
    take = lambda count: [refs.pop(0) for _ in range(count)]
    kron_ref = take(1)[0]
    coming = [] if is_last else take(4)
    given = take(4) if is_first else take(2)
    take(waits)
    factors_ref = take(1)[0] if gathers else None
    keep_ref, send_ref = take(2)
    handed = [] if is_last else take(2)
    gathered = take(len(gathers))
    turned_first, turned_second, integral, total, sems = take(5)
    staged, load_sems, store_sems = take(3) if gathers else (None, None, None)
    turned = (turned_first, turned_second)
    step = pl.program_id(0)
    ends = pl.num_programs(0) - 1
    now = lax.rem(step, 2)
    later = 1 - now
    blocks = WIDTH // ROWS
    places = (0, DEPTH)

    loads, stores = [], []
    for group, (begin, count) in zip(gathered, gathers):
        for t in range(count):
            for side in range(2):
                n = len(loads)
                source = factors_ref.at[plan[(layout.partner_first, layout.partner_second)[side] + begin + t]]
                loads.append(pltpu.make_async_copy(source, staged.at[n], load_sems.at[n]))
                stores.append(pltpu.make_async_copy(staged.at[n], group.at[t, side], store_sems.at[n]))
    for load in loads:
        load.start()

    @pl.when(step == 0)
    def _():
        if is_first:
            blank = jnp.zeros((2, window * WIDTH, DEPTH - rows), jnp.bfloat16)
            for which in range(2):
                for half, place in enumerate(places):
                    turned[which][:, :, place + rows : place + DEPTH] = blank
                    for d in range(window):
                        turn_columns(given[2 * which + half], turned[which], 0, d, place)
        else:
            takes = [pltpu.make_async_copy(given[i], turned[i].at[0], sems.at[i]) for i in range(2)]
            for copy in takes:
                copy.start()
            if not is_last:
                blank = jnp.zeros((window * WIDTH, DEPTH - rows), jnp.bfloat16)
                for which in range(2):
                    for place in places:
                        turned[which][1, :, place + rows : place + DEPTH] = blank
            for copy in takes:
                copy.wait()

    def hand_on(i):
        return pltpu.make_async_copy(turned[i].at[later], handed[i], sems.at[2 + i])

    def one_block(block, carry):
        pieces = []
        for part in range(TOGETHER):
            start = pl.multiple_of((block * TOGETHER + part) * ROWS, ROWS)
            pieces += [turned_first[now, pl.ds(c * WIDTH + start, ROWS), :] for c in range(window)]
            pieces.append(jnp.zeros((DEPTH - window * ROWS, 2 * DEPTH), jnp.bfloat16))
        right = jnp.concatenate(pieces, axis=0)
        product = lax.dot_general(
            turned_second[now], right, (((1,), (1,)), ((), ())), preferred_element_type=jnp.float32
        )
        if not is_last:
            rounds = blocks // TOGETHER
            for d in range(pl.cdiv(window, rounds)):
                for half in range(2):
                    turn_columns(
                        coming[half], turned_first, later, jnp.minimum(block + d * rounds, window - 1), places[half]
                    )
        for part in range(TOGETHER):
            integral[block * TOGETHER + part] = product[:, part * DEPTH : (part + 1) * DEPTH].astype(jnp.bfloat16)
        return carry

    lax.fori_loop(0, blocks // TOGETHER, one_block, 0)
    for load, store in zip(loads, stores):
        load.wait()
        store.start()
    if not is_last:

        @pl.when(step == ends)
        def _():
            hand_on(0).start()

    for d in range(0, window, STEP):
        parts = range(d, min(d + STEP, window))
        left = jnp.concatenate(
            [integral[:, e * WIDTH : (e + 1) * WIDTH, :].reshape(blocks * WIDTH, DEPTH) for e in parts], axis=1
        )
        product = jnp.dot(
            left, kron_ref[d * DEPTH : (d + len(parts)) * DEPTH, :], preferred_element_type=jnp.float32
        )
        if not is_last:
            for e in parts:
                for half in range(2):
                    turn_columns(coming[2 + half], turned_second, later, e, places[half])
        if d == 0:
            total[...] = product
        else:
            total[...] += product

    for block in range(blocks):
        lines = slice(block * WIDTH, (block + 1) * WIDTH)
        keep_ref[0, block] = total[lines, :WIDTH].astype(jnp.bfloat16)
        send_ref[0, block] = total[lines, WIDTH:].astype(jnp.bfloat16)

    if not is_last:

        @pl.when(step == ends)
        def _():
            hand_on(1).start()
            hand_on(0).wait()
            hand_on(1).wait()

    for store in stores:
        store.wait()


def partial_ladders(plan, layout, begin, tiles, factors, partner, kron, given, window, waits, gathers, is_last):
    rows, columns = factors.shape[1:]
    blocks = WIDTH // ROWS
    side = (1, rows, columns)
    once = pl.Buffered(1)
    turned_shape = (columns, 2 * DEPTH)
    is_first = given is None
    first, second = layout.own_first + begin, layout.own_second + begin
    operands = [kron]
    in_specs = [pl.BlockSpec(kron.shape, lambda j, p: (0, 0), pipeline_mode=once)]
    skip = 1 if is_first else 0
    if not is_last:
        operands += [factors, partner, factors, partner]
        in_specs += [
            pl.BlockSpec(side, lambda j, p: (p[first + j + 1], 0, 0)),
            pl.BlockSpec((1,) + side, lambda j, p: (j + skip, 0, 0, 0)),
            pl.BlockSpec(side, lambda j, p: (p[second + j + 1], 0, 0)),
            pl.BlockSpec((1,) + side, lambda j, p: (j + skip, 1, 0, 0)),
        ]
    if is_first:
        operands += [factors, partner, factors, partner]
        in_specs += [
            pl.BlockSpec(side, lambda j, p: (p[first], 0, 0), pipeline_mode=once),
            pl.BlockSpec((1,) + side, lambda j, p: (0, 0, 0, 0), pipeline_mode=once),
            pl.BlockSpec(side, lambda j, p: (p[second], 0, 0), pipeline_mode=once),
            pl.BlockSpec((1,) + side, lambda j, p: (0, 1, 0, 0), pipeline_mode=once),
        ]
    else:
        operands += list(given)
        in_specs += [HBM] * 2
    operands += list(waits)
    in_specs += [HBM] * len(waits)
    if gathers:
        operands.append(factors)
        in_specs.append(HBM)
    part_spec = pl.BlockSpec((1, blocks, WIDTH, WIDTH), lambda j, p: (j, 0, 0, 0))
    part = jax.ShapeDtypeStruct((tiles, blocks, WIDTH, WIDTH), jnp.bfloat16)
    out_specs, out_shape = [part_spec, part_spec], [part, part]
    if not is_last:
        out_specs += [HBM] * 2
        out_shape += [jax.ShapeDtypeStruct(turned_shape, jnp.bfloat16)] * 2
    out_specs += [HBM] * len(gathers)
    out_shape += [jax.ShapeDtypeStruct((count, 2, rows, columns), jnp.bfloat16) for _, count in gathers]
    scratch_shapes = [
        pltpu.VMEM((2,) + turned_shape, jnp.bfloat16),
        pltpu.VMEM((2,) + turned_shape, jnp.bfloat16),
        pltpu.VMEM((blocks, columns, DEPTH), jnp.bfloat16),
        pltpu.VMEM((blocks * WIDTH, kron.shape[1]), jnp.float32),
        pltpu.SemaphoreType.DMA((4,)),
    ]
    if gathers:
        sides = 2 * sum(count for _, count in gathers)
        scratch_shapes += [
            pltpu.VMEM((sides, rows, columns), jnp.bfloat16),
            pltpu.SemaphoreType.DMA((sides,)),
            pltpu.SemaphoreType.DMA((sides,)),
        ]
    flops = tiles * 6 * columns * DEPTH * blocks * DEPTH
    return pl.pallas_call(
        functools.partial(
            partial_kernel,
            layout=layout,
            window=window,
            rows=rows,
            is_first=is_first,
            is_last=is_last,
            waits=len(waits),
            gathers=gathers,
        ),
        grid_spec=pltpu.PrefetchScalarGridSpec(
            num_scalar_prefetch=1,
            grid=(tiles,),
            in_specs=in_specs,
            out_specs=out_specs,
            scratch_shapes=scratch_shapes,
        ),
        out_shape=out_shape,
        compiler_params=pltpu.CompilerParams(vmem_limit_bytes=LADDER_VMEM),
        cost_estimate=pl.CostEstimate(
            flops=flops, bytes_accessed=tiles * 4 * rows * columns * 2 + kron.size * 2, transcendentals=0
        ),
    )(plan, *operands)


def gather_kernel(plan, factors_ref, out_ref, staged, load_sems, store_sems, *, layout, begin):
    loads, stores = [], []
    for t in range(out_ref.shape[0]):
        for side, start in enumerate((layout.partner_first, layout.partner_second)):
            n = len(loads)
            source = factors_ref.at[plan[start + begin + t]]
            loads.append(pltpu.make_async_copy(source, staged.at[n], load_sems.at[n]))
            stores.append(pltpu.make_async_copy(staged.at[n], out_ref.at[t, side], store_sems.at[n]))
    for load in loads:
        load.start()
    for load, store in zip(loads, stores):
        load.wait()
        store.start()
    for store in stores:
        store.wait()


def gather(plan, layout, factors, begin, count):
    rows, columns = factors.shape[1:]
    return pl.pallas_call(
        functools.partial(gather_kernel, layout=layout, begin=begin),
        grid_spec=pltpu.PrefetchScalarGridSpec(
            num_scalar_prefetch=1,
            grid=(1,),
            in_specs=[HBM],
            out_specs=HBM,
            scratch_shapes=[
                pltpu.VMEM((2 * count, rows, columns), factors.dtype),
                pltpu.SemaphoreType.DMA((2 * count,)),
                pltpu.SemaphoreType.DMA((2 * count,)),
            ],
        ),
        out_shape=jax.ShapeDtypeStruct((count, 2, rows, columns), factors.dtype),
        compiler_params=pltpu.CompilerParams(vmem_limit_bytes=GATHER_VMEM),
    )(plan, factors)


def combine_kernel(*refs, counts):
    ins, outs = refs[: sum(counts)], refs[sum(counts) + 1 :]
    begin = 0
    for count, out in zip(counts, outs):
        for block in range(out.shape[1]):
            value = ins[begin][0, block].astype(jnp.float32)
            for ref in ins[begin + 1 : begin + count]:
                value = value + ref[0, block].astype(jnp.float32)
            out[0, block] = value.astype(out.dtype)
        begin += count


def combine(groups, after):
    def at(place, shape):
        return pl.BlockSpec((1,) + shape[1:], lambda i: (place, 0, 0, 0))

    shape = groups[0][0][0].shape
    return pl.pallas_call(
        functools.partial(combine_kernel, counts=tuple(len(group) for group in groups)),
        grid=(1,),
        in_specs=[at(place, array.shape) for group in groups for array, place in group] + [HBM],
        out_specs=[at(0, shape)] * len(groups),
        out_shape=[jax.ShapeDtypeStruct((1,) + shape[1:], jnp.bfloat16)] * len(groups),
        compiler_params=pltpu.CompilerParams(vmem_limit_bytes=SMALL_VMEM),
    )(*[array for group in groups for array, _ in group], after)


def prepare_kernel(plan, residual_ref, out_ref, token_ref, held_ref, blank, put_sems, load_sems, *, layout):
    blank[...] = jnp.zeros_like(blank)
    token_ref[...] = jnp.zeros_like(token_ref)

    def put(i):
        return pltpu.make_async_copy(blank, out_ref.at[i], put_sems.at[i])

    def load(t):
        return pltpu.make_async_copy(residual_ref.at[plan[layout.arrive + t]], held_ref.at[t], load_sems.at[t])

    for i in range(out_ref.shape[0]):

        @pl.when(plan[layout.filled + i] == 0)
        def _():
            put(i).start()

    for t in range(held_ref.shape[0]):

        @pl.when(plan[layout.arrive + t] >= 0)
        def _():
            load(t).start()

    for i in range(out_ref.shape[0]):

        @pl.when(plan[layout.filled + i] == 0)
        def _():
            put(i).wait()

    for t in range(held_ref.shape[0]):

        @pl.when(plan[layout.arrive + t] >= 0)
        def _():
            load(t).wait()


def prepare(plan, layout, residual, tiles):
    grid_spec = pltpu.PrefetchScalarGridSpec(
        num_scalar_prefetch=1,
        grid=(1,),
        in_specs=[HBM],
        out_specs=[
            HBM,
            pl.BlockSpec((8, WIDTH), lambda i, p: (0, 0)),
            pl.BlockSpec((tiles,) + residual.shape[1:], lambda i, p: (0, 0, 0), pipeline_mode=pl.Buffered(1)),
        ],
        scratch_shapes=[
            pltpu.VMEM(residual.shape[1:], residual.dtype),
            pltpu.SemaphoreType.DMA((residual.shape[0],)),
            pltpu.SemaphoreType.DMA((tiles,)),
        ],
    )
    return pl.pallas_call(
        functools.partial(prepare_kernel, layout=layout),
        grid_spec=grid_spec,
        out_shape=[
            jax.ShapeDtypeStruct(residual.shape, residual.dtype),
            jax.ShapeDtypeStruct((8, WIDTH), jnp.float32),
            jax.ShapeDtypeStruct((tiles,) + residual.shape[1:], residual.dtype),
        ],
        compiler_params=pltpu.CompilerParams(vmem_limit_bytes=GATHER_VMEM),
    )(plan, residual)


def finish_kernel(plan, *refs, layout):
    parts, (keep_ref, send_ref, turned) = refs[:-3], refs[-3:]
    pairs = keep_ref.shape[0]
    half = plan[layout.half]
    mine = half * pairs * ROWS
    other = (1 - half) * pairs * ROWS
    for block in range(WIDTH // ROWS):
        value = parts[0][0, block].astype(jnp.float32)
        for part in parts[1:]:
            value = value + part[0, block].astype(jnp.float32)
        turned[block] = value.T
        for row in range(ROWS):
            lanes = slice((block * ROWS + row) * WIDTH, (block * ROWS + row + 1) * WIDTH)
            for start, ref in ((mine, keep_ref), (other, send_ref)):
                piece = turned[block, pl.ds(start + row, pairs, stride=ROWS), :]
                ref[:, lanes] = piece.astype(jnp.bfloat16)


def finish(plan, layout, parts, pairs):
    out = jax.ShapeDtypeStruct((pairs, WIDTH * WIDTH), jnp.bfloat16)
    return pl.pallas_call(
        functools.partial(finish_kernel, layout=layout),
        grid_spec=pltpu.PrefetchScalarGridSpec(
            num_scalar_prefetch=1,
            grid=(1,),
            in_specs=[pl.BlockSpec(part.shape, lambda i, h: (0, 0, 0, 0)) for part in parts],
            out_specs=[pl.BlockSpec(out.shape, lambda i, h: (0, 0))] * 2,
            scratch_shapes=[pltpu.VMEM((WIDTH // ROWS, WIDTH, WIDTH), jnp.float32)],
        ),
        out_shape=[out, out],
        compiler_params=pltpu.CompilerParams(vmem_limit_bytes=SMALL_VMEM),
    )(plan, *parts)


def pick_kernel(plan, own_ref, other_ref, *slot_refs, layout):
    for k, slot_ref in enumerate(slot_refs):

        @pl.when(plan[layout.pick + 1 + k] == 0)
        def _():
            slot_ref[...] = own_ref[...]

        @pl.when(plan[layout.pick + 1 + k] != 0)
        def _():
            slot_ref[...] = other_ref[...]


def pick(plan, layout, own, other, slots):
    whole = pl.BlockSpec(own.shape, lambda i, p: (0, 0))
    return pl.pallas_call(
        functools.partial(pick_kernel, layout=layout),
        grid_spec=pltpu.PrefetchScalarGridSpec(
            num_scalar_prefetch=1,
            grid=(1,),
            in_specs=[whole, whole],
            out_specs=[whole] * slots,
        ),
        out_shape=[jax.ShapeDtypeStruct(own.shape, own.dtype)] * slots,
        compiler_params=pltpu.CompilerParams(vmem_limit_bytes=SMALL_VMEM),
    )(plan, own, other)


def squares_kernel(plan, own_ref, other_ref, after_ref, mean_ref, *, layout):
    pairs, columns = own_ref.shape
    half = plan[layout.half]
    lane = lax.broadcasted_iota(jnp.int32, (pairs, WIDTH), 1)
    means = jnp.zeros((pairs, WIDTH), jnp.float32)
    for i, ref in enumerate((own_ref, other_ref)):
        squares = jnp.zeros((pairs, WIDTH), jnp.float32)
        for a in range(columns // WIDTH):
            squares = squares + jnp.square(ref[:, a * WIDTH : (a + 1) * WIDTH].astype(jnp.float32))
        mean = jnp.sum(squares, axis=1, keepdims=True) / columns
        means = jnp.where(lane == jnp.where(half == 0, i, 1 - i), mean, means)
    mean_ref[...] = means


def mean_squares(plan, layout, own, other, after):
    whole = pl.BlockSpec(own.shape, lambda i, p: (0, 0))
    out = jax.ShapeDtypeStruct((own.shape[0], WIDTH), jnp.float32)
    return pl.pallas_call(
        functools.partial(squares_kernel, layout=layout),
        grid_spec=pltpu.PrefetchScalarGridSpec(
            num_scalar_prefetch=1,
            grid=(1,),
            in_specs=[whole, whole, HBM],
            out_specs=pl.BlockSpec(out.shape, lambda i, p: (0, 0)),
        ),
        out_shape=out,
        compiler_params=pltpu.CompilerParams(vmem_limit_bytes=SMALL_VMEM),
    )(plan, own, other, after)


def home_kernel(plan, cleared_ref, held_ref, *refs, layout):
    tiles = held_ref.shape[0]
    ladders, (out_ref, total, sems) = refs[:tiles], refs[tiles:]

    def store(t):
        return pltpu.make_async_copy(total.at[t], out_ref.at[plan[layout.arrive + t]], sems.at[t])

    for t in range(tiles):

        @pl.when(plan[layout.arrive + t] >= 0)
        def _():
            value = held_ref[t].astype(jnp.float32) + ladders[t][...].astype(jnp.float32)
            total[t] = value.astype(total.dtype)
            store(t).start()

    for t in range(tiles):

        @pl.when(plan[layout.arrive + t] >= 0)
        def _():
            store(t).wait()


def add_at_home(plan, layout, cleared, held, ladders):
    tiles = held.shape[0]
    grid_spec = pltpu.PrefetchScalarGridSpec(
        num_scalar_prefetch=1,
        grid=(1,),
        in_specs=[HBM, pl.BlockSpec(held.shape, lambda i, s: (0, 0, 0))]
        + [pl.BlockSpec(ladder.shape, lambda i, s: (0, 0)) for ladder in ladders],
        out_specs=HBM,
        scratch_shapes=[pltpu.VMEM(held.shape, held.dtype), pltpu.SemaphoreType.DMA((tiles,))],
    )
    return pl.pallas_call(
        functools.partial(home_kernel, layout=layout),
        grid_spec=grid_spec,
        out_shape=jax.ShapeDtypeStruct(cleared.shape, cleared.dtype),
        input_output_aliases={1: 0},
        compiler_params=pltpu.CompilerParams(vmem_limit_bytes=SMALL_VMEM),
    )(plan, cleared, held, *ladders)


def kron_factor(t2_window, flip):
    pairs, window = t2_window.shape[:2]
    padded = DEPTH // ROWS
    terms = window * padded
    by_term = jnp.pad(t2_window, ((0, 0), (0, padded - window), (0, 0))).transpose(2, 1, 0).reshape(terms, pairs)
    columns = jnp.arange(pairs * ROWS, dtype=jnp.int32)
    rows = jnp.arange(terms * ROWS, dtype=jnp.int32)
    pick_pair = (jnp.arange(pairs, dtype=jnp.int32)[:, None] == ((columns // ROWS) ^ flip)[None, :]).astype(
        jnp.bfloat16
    )
    pick_term = (rows[:, None] // ROWS == jnp.arange(terms, dtype=jnp.int32)[None, :]).astype(jnp.bfloat16)
    by_column = jnp.dot(by_term, pick_pair, preferred_element_type=jnp.float32).astype(jnp.bfloat16)
    wide = jnp.dot(pick_term, by_column, preferred_element_type=jnp.float32).astype(jnp.bfloat16)
    return jnp.where(rows[:, None] % ROWS == columns[None, :] % ROWS, wide, jnp.zeros((), jnp.bfloat16))


def exchange(value, axis, bit):
    count = lax.axis_size(axis)
    return lax.ppermute(value, axis, [(i, i ^ bit) for i in range(count)])


def sending_order(owner_count):
    names = sorted(range(owner_count), key=lambda name: (-bin(name).count("1"), -name))
    if owner_count > 4:
        high = owner_count // 2
        names.remove(high)
        names.insert(len(names) - 3, high)
    return names


def body(factors, t2_window, residual_in, tile_mask, owner_slot, home_slot):
    owner_count = lax.axis_size("wide")
    narrow_count = lax.axis_size("narrow")
    wide = lax.axis_index("wide")
    narrow = lax.axis_index("narrow")
    pairs, window = t2_window.shape[:2]
    own_pairs = pairs // narrow_count
    home_count = residual_in.shape[0]
    half = narrow % 2
    names = sending_order(owner_count)
    layout = Layout(owner_count, home_count)
    place = jnp.stack([wide, half]).astype(jnp.int32)
    plan = make_plan(place, tile_mask, owner_slot, home_slot, layout, names, factors.shape[0], home_count)

    most = max(1, owner_count // 4)
    ends = [1] + list(range(1 + most, owner_count - 1, most)) + [owner_count - 1, owner_count]
    begins = [0] + ends[:-1]
    last = len(ends) - 1
    group_ranges = [(0, 2)] + [(begin + 1, end - begin) for begin, end in zip(begins[1:-1], ends[1:-1])]

    def exchange_rows(value):
        return exchange(value, "narrow", 1)

    partner_rows = [exchange_rows(gather(plan, layout, factors, *group)) for group in group_ranges[:2]]
    kron = kron_factor(t2_window, narrow // 2 * (SLOTS * own_pairs))
    cleared, token, held = prepare(plan, layout, residual_in, owner_count + 1)
    arrived = {w: [] for w in range(owner_count)}
    summed = {}
    unsent = [w for w in names if w]
    given, parts = None, []

    def send_wide(calls):
        for i in range(calls):
            for place, w in enumerate(names[begins[i] : ends[i]]):
                summed.setdefault(w, [(parts[i][0], place), (parts[i][1], place)])
        ready = [w for w in unsent if w in summed and len(arrived[w]) == (w & -w).bit_length() - 1]
        if not ready:
            return []
        sent = combine([summed[w] + [(value, 0) for value in arrived[w]] for w in ready], parts[-1][0])
        for w, value in zip(ready, sent):
            unsent.remove(w)
            arrived[w & (w - 1)].append(exchange(value, "wide", w & -w))
        return list(sent)

    for i in range(last + 1):
        waits = send_wide(i - 1) if i else [token]
        keep, send, *rest = partial_ladders(
            plan,
            layout,
            begins[i],
            ends[i] - begins[i],
            factors,
            partner_rows[i] if i < last else None,
            kron,
            given,
            window,
            waits,
            tuple(group_ranges[2:]) if i == 0 else (),
            i == last,
        )
        given = rest[:2]
        partner_rows += [exchange_rows(group) for group in rest[2:]]
        parts.append((keep, exchange(send, "narrow", 2)))
    while unsent:
        send_wide(last + 1)

    keep, send = finish(plan, layout, list(parts[last]) + arrived[0], own_pairs)
    other = exchange(send, "narrow", 1)
    slots = pick(plan, layout, keep, other, owner_count - 1)
    near = owner_count // 2
    came = [exchange(slots[k - 1], "wide", k) for k in range(near, 0, -1)][::-1]

    def from_far(*values):
        return tuple(exchange(value, "wide", near + 1 + k) for k, value in enumerate(values))

    def from_none(*values):
        return tuple(jnp.zeros_like(value) for value in values)

    if owner_count - 1 > near:
        came += lax.cond(plan[layout.matched] == 1, from_none, from_far, *slots[near:])

    norms = mean_squares(plan, layout, keep, other, came[0])[:, :SLOTS].T
    for bit in range(owner_count.bit_length() - 1):
        norms = jnp.concatenate([norms, exchange(norms, "wide", 1 << bit)], axis=0)
    rows = plan[layout.norm : layout.norm + SLOTS]
    here = rows[:, None] == jnp.arange(norms.shape[0], dtype=jnp.int32)[None, :]
    ladder_norms = jnp.sum(jnp.where(here[:, :, None], norms[None], 0.0), axis=1)
    residual_out = add_at_home(plan, layout, cleared, held, [keep, other] + came)
    return (residual_out, ladder_norms)


def solution(mesh):
    in_specs = (P(None, ("wide", "narrow"), None), P(), P("wide", "narrow", None), P(), P(), P())
    out_specs = (P("wide", "narrow", None), P("wide", "narrow"))
    return jax.shard_map(body, mesh=mesh, in_specs=in_specs, out_specs=out_specs, check_vma=False)
```

time: 966 us -> 179 us (0.19)
  waiting for transfers between devices: 641 us -> 23.7 us
  local copies, waits for them, and re-layouts: 117 us -> 5.01 us
  Pallas kernels: 0 us -> 108 us
  matrix products: 92 us -> 2.5 us
  blocking collectives: 40.1 us -> 0 us
  loops' own time: 29.2 us -> 0.01 us
  starting transfers between devices: 7.46 us -> 35.9 us
  other arithmetic: 21.5 us -> 1.75 us
  between operations: 15 us -> 1.58 us
    all_to_all x1 -> x0, waiting for transfers between devices: 593 us -> none  [body(): lax.all_to_all(outgoing, 'wide', split_axis=0, concat_axis=0, tiled=True)]
    pallas_call x0 -> x17, Pallas kernels: none -> 108 us  [the longest x5 88 us: partial_ladders(): pl.pallas_call(functools.partial(partial_kernel, layout=layout, window=wi...]
    dot_general x5 -> x1, matrix products: 92 us -> 2.5 us  [kron_factor(): jnp.dot(pick_term, by_column, preferred_element_type=jnp.float32)]
    all_gather x1 -> x0, waiting for transfers between devices: 47.3 us -> none  [body(): gathered_rows = lax.all_gather(ladder, 'wide', axis=0, tiled=True)]
    unnamed x1 -> x0, blocking collectives: 40.1 us -> none
    dot_general x6 -> x0, local copies, waits for them, and re-layouts: 40.1 us -> none  [the longest x4 39.4 us: tile_contract(): lax.dot_general(first_side, second_side, (((0,), (0,)), ((), ())), prefer...]
    ppermute x0 -> x27, starting transfers between devices: none -> 35.9 us  [exchange(): return lax.ppermute(value, axis, [(i, i ^ bit) for i in range(count)])]
    another operation x1, loops' own time: 29.2 us -> 0.01 us  [body(): lax.cond(plan[layout.matched] == 1, from_none, from_far, *slots[near:])]
  transfers between devices with their start and end apart: 2 -> 27, of which waited for: 2 -> 8; matrix products, arithmetic and copies ran while one was open for 0% -> 2% of each run, Pallas kernels for 0% -> 55%
where the time goes in v1:
time: 179 us
  Pallas kernels  108 us (60%)
  starting transfers between devices  35.9 us (20%)
  waiting for transfers between devices  23.7 us (13%)
  local copies, waits for them, and re-layouts  5.01 us (3%)
  matrix products  2.5 us (1%)
    pallas_call x5, Pallas kernels, partial_ladders(): pl.pallas_call(functools.partial(partial_kernel, layout=layout, window=wi...  88 us
    ppermute x27, starting transfers between devices, exchange(): return lax.ppermute(value, axis, [(i, i ^ bit) for i in range(count)])  35.9 us
    ppermute x27, waiting for transfers between devices, exchange(): return lax.ppermute(value, axis, [(i, i ^ bit) for i in range(count)])  23.7 us
    pallas_call x2, Pallas kernels, gather(): pl.pallas_call(functools.partial(gather_kernel, layout=layout, begin=begi...  7.93 us
    pallas_call x1, Pallas kernels, make_plan(): pl.pallas_call(functools.partial(plan_kernel, layout=layout, names=names,...  4.34 us
    unnamed x14, local copies, waits for them, and re-layouts  4.02 us
    pallas_call x1, Pallas kernels, prepare(): pl.pallas_call(functools.partial(prepare_kernel, layout=layout), grid_spe...  3.79 us
  transfers between devices with their start and end apart: 27, of which 8 were waited for; matrix products, arithmetic and copies ran while one was open for 2% of the time, Pallas kernels for 55%

profile of v1, /device:TPU:0, one launch (start us, length us, event | category | flops | bytes accessed | tf_op | source)
XLA Modules:
  0.0 178.8 jit_solution(5530588021324566924)
XLA Ops:
  1.4 4.3 %shard_map.77.plan = s32[82]{0:T(128)S(1)} custom-call(s32[2]{0:T(128)S(1)} %pad_add_fusion.place, s32[225]{0:T(256)S(1)} %multiply_add_fusion.table), custom_call_target="tpu_custom_call" | custom-call | tf_op jit(solution)/shard_map/pallas_call | solution.py:212
  6.3 3.6 %shard_map.79 = bf16[2,2,224,1920]{3,2,1,0:T(8,128)(2,1)} custom-call(s32[82]{0:T(128)} %copy-done.1, bf16[15,224,1920]{2,1,0:T(8,128)(2,1)} %refs_3_.7), custom_call_target="tpu_custom_call" | custom-call | tf_op jit(solution)/shard_map/pallas_call | solution.py:453
  11.2 4.3 %shard_map.81 = bf16[2,2,224,1920]{3,2,1,0:T(8,128)(2,1)} custom-call(s32[82]{0:T(128)} %copy-done.1, bf16[15,224,1920]{2,1,0:T(8,128)(2,1)} %refs_3_.7), custom_call_target="tpu_custom_call" | custom-call | tf_op jit(solution)/shard_map/pallas_call | solution.py:453
  15.6 3.8 %shard_map.78 = (bf16[29,4,16384]{2,1,0:T(4,128)(2,1)}, f32[8,128]{1,0:T(8,128)}, bf16[9,4,16384]{2,1,0:T(4,128)(2,1)}) custom-call(s32[82]{0:T(128)} %copy-done.1, bf16[29,4,16384]{2,1,0:T(4,128)(2,1)} %residual_ref.1), custom_call_target="tpu_custom_call" | custom-call | tf_op jit(solution)/shard_map/pallas_call | solution.py:549
  19.8 2.5 %fusion.refs_0_ = bf16[3840,256]{1,0:T(8,128)(2,1)} fusion(s32[3840]{0:T(1024)S(1)} %get-tuple-element.93, s32[256]{0:T(256)S(1)} %get-tuple-element.95, s32[3840]{0:T(1024)S(1)} %get-tuple-element.94, bf16[240,16]{0,1:T(8,128)(2,1)S(1)} %reshape.114, s32[256]{0:T(256)S(1)} %get-tuple-element.96), kind=kOutput, calls=%fused_computation.1 | convolution fusion | flops 477761536 | bytes 2006528 | tf_op jit(solution)/shard_map/dot_general | solution.py:705
  22.3 14.5 %shard_map.80 = (bf16[1,8,128,128]{3,2,1,0:T(8,128)(2,1)S(1)}, bf16[1,8,128,128]{3,2,1,0:T(8,128)(2,1)S(1)}, bf16[1920,512]{1,0:T(8,128)(2,1)}, bf16[1920,512]{1...) custom-call(s32[82]{0:T(128)S(1)} %copy-done.2, bf16[3840,256]{1,0:T(8,128)(2,1)} %fusion.refs_0_, ...), custom_call_target="tpu_custom_call" | custom-call | flops 6039797760 | bytes 5406720 | tf_op jit(solution)/shard_map/pallas_call | solution.py:408
  37.4 2.3 %collective-permute-start.7 = (bf16[1,8,128,128]{3,2,1,0:T(8,128)(2,1)S(1)}, bf16[1,8,128,128]{3,2,1,0:T(8,128)(2,1)S(1)}, u32[]{:S(2)}, u32[]{:S(2)}) collective-permute-start(bf16[1,8,128,128]{3,2,1,0:T(8,128)(2,1)S(1)} %get-tuple-element.62), channel_id=1, source_target_pairs={{0,2},{1,3},{2,0},{3,1},{4,6},{5,7},{6,4},{7,5},{8,10},{9,11},{10,... | collective-permute-start | bytes 786440 | tf_op jit(solution)/shard_map/ppermute | solution.py:711
  39.8 20.7 %shard_map.82 = (bf16[2,8,128,128]{3,2,1,0:T(8,128)(2,1)S(1)}, bf16[2,8,128,128]{3,2,1,0:T(8,128)(2,1)S(1)}, bf16[1920,512]{1,0:T(8,128)(2,1)}, bf16[1920,512]{1,0:T(8,128)(2,1)}) custom-call(s32[82]{0:T(128)S(1)} %copy-done.2, bf16[3840,256]{1,0:T(8,128)(2,1)} %fusion.refs_0_, bf16[15,224,1920]{2,1,0:T(8,128)(2,1)} %refs_3_.7, ...), custom_call_target="tpu_custom_call" | custom-call | flops 12079595520 | bytes 8847360 | tf_op jit(solution)/shard_map/pallas_call | solution.py:408
  62.3 1.8 copy-done.6
  64.0 20.9 %shard_map.84 = (bf16[2,8,128,128]{3,2,1,0:T(8,128)(2,1)S(1)}, bf16[2,8,128,128]{3,2,1,0:T(8,128)(2,1)S(1)}, bf16[1920,512]{1,0:T(8,128)(2,1)}, bf16[1920,512]{1,0:T(8,128)(2,1)}) custom-call(s32[82]{0:T(128)S(1)} %copy-done.2, bf16[3840,256]{1,0:T(8,128)(2,1)} %fusion.refs_0_, bf16[15,224,1920]{2,1,0:T(8,128)(2,1)} %refs_3_.7, ...), custom_call_target="tpu_custom_call" | custom-call | flops 12079595520 | bytes 8847360 | tf_op jit(solution)/shard_map/pallas_call | solution.py:408
  88.1 1.9 %collective-permute-start.12 = (bf16[1,8,128,128]{3,2,1,0:T(8,128)(2,1)S(1)}, bf16[1,8,128,128]{3,2,1,0:T(8,128)(2,1)S(1)}, u32[]{:S(2)}, u32[]{:S(2)}) collective-permute-start(bf16[1,8,128,128]{3,2,1,0:T(8,128)(2,1)S(1)} %get-tuple-element.69.refs_8_), channel_id=1, source_target_pairs={{0,4},{4,0},{8,12},{12,8},{16,20},{20,16},{24,28},{28,24},{1,5},{5... | collective-permute-start | bytes 786440 | tf_op jit(solution)/shard_map/ppermute | solution.py:711
  91.7 20.8 %shard_map.86 = (bf16[2,8,128,128]{3,2,1,0:T(8,128)(2,1)S(1)}, bf16[2,8,128,128]{3,2,1,0:T(8,128)(2,1)S(1)}, bf16[1920,512]{1,0:T(8,128)(2,1)}, bf16[1920,512]{1,0:T(8,128)(2,1)}) custom-call(s32[82]{0:T(128)S(1)} %copy-done.2, bf16[3840,256]{1,0:T(8,128)(2,1)} %fusion.refs_0_, bf16[15,224,1920]{2,1,0:T(8,128)(2,1)} %refs_3_.7, ...), custom_call_target="tpu_custom_call" | custom-call | flops 12079595520 | bytes 8847360 | tf_op jit(solution)/shard_map/pallas_call | solution.py:408
  114.8 2.0 %collective-permute-start.16 = (bf16[1,8,128,128]{3,2,1,0:T(8,128)(2,1)S(1)}, bf16[1,8,128,128]{3,2,1,0:T(8,128)(2,1)S(1)}, u32[]{:S(2)}, u32[]{:S(2)}) collective-permute-start(bf16[1,8,128,128]{3,2,1,0:T(8,128)(2,1)S(1)} %get-tuple-element.74.refs_3_), channel_id=1, source_target_pairs={{0,4},{4,0},{8,12},{12,8},{16,20},{20,16},{24,28},{28,24},{1,5},{5... | collective-permute-start | bytes 786440 | tf_op jit(solution)/shard_map/ppermute | solution.py:711
  116.8 11.1 %shard_map.88 = (bf16[1,8,128,128]{3,2,1,0:T(8,128)(2,1)S(1)}, bf16[1,8,128,128]{3,2,1,0:T(8,128)(2,1)S(1)}) custom-call(s32[82]{0:T(128)S(1)} %copy-done.2, bf16[3840,256]{1,0:T(8,128)(2,1)} %fusion.refs_0_, bf16[1920,512]{1,0:T(8,128)(2,1)} %get-tuple-element.70.refs_1_, bf16[1920,512]{1,0:T(8,128)(2,1)} %get-tuple-element.71.refs_2_, ...), custom_call_target="tpu_custom_call" | custom-call | flops 6039797760 | bytes 5406720 | tf_op jit(solution)/shard_map/pallas_call | solution.py:408
  130.1 4.2 %collective-permute-done.13.refs_1_ = bf16[1,8,128,128]{3,2,1,0:T(8,128)(2,1)S(1)} collective-permute-done((bf16[1,8,128,128]{3,2,1,0:T(8,128)(2,1)S(1)}, bf16[1,8,128,128]{3,2,1,0:T(8,128)(2,1)S(1)}, u32[]{:S(2)}, u32[]{:S(2)}) %collective-permute-start.13) | collective-permute-done | bytes 262176 | tf_op jit(solution)/shard_map/ppermute | solution.py:711
  134.3 1.7 collective-permute-done.17.refs_3_
  142.6 15.8 %conditional.1 = (bf16[4,16384]{1,0:T(4,128)(2,1)S(1)}, bf16[4,16384]{1,0:T(4,128)(2,1)S(1)}, bf16[4,16384]{1,0:T(4,128)(2,1)S(1)}) conditional(s32[]{:T(128)} %bitcast.3, (bf16[4,16384]{1,0:T(4,128)(2,1)S(1)}, bf16[4,16384]{1,0:T(4,128)(2,1)S(1)}, bf16[4,16384]{1,0:T(4,128)(2,1)S(1)}) %tuple.16, () %tuple.17), branch_computations={%region_0.1_spmd, %region_1.2_spmd} | conditional | bytes 1573008 | solution.py:802
  144.1 2.4 %collective-permute-start.1 = (bf16[4,16384]{1,0:T(4,128)(2,1)S(1)}, bf16[4,16384]{1,0:T(4,128)(2,1)S(1)}, u32[]{:S(2)}, u32[]{:S(2)}) collective-permute-start(bf16[4,16384]{1,0:T(4,128)(2,1)S(1)} %get-tuple-element.7), channel_id=1, source_target_pairs={{0,24},{4,28},{8,16},{12,20},{16,8},{20,12},{24,0},{28,4},{1,25},{... | collective-permute-start | bytes 393224 | tf_op jit(solution)/shard_map/cond/branch_0_fun/ppermute | solution.py:711
  146.5 2.4 %collective-permute-start.2 = (bf16[4,16384]{1,0:T(4,128)(2,1)S(1)}, bf16[4,16384]{1,0:T(4,128)(2,1)S(1)}, u32[]{:S(2)}, u32[]{:S(2)}) collective-permute-start(bf16[4,16384]{1,0:T(4,128)(2,1)S(1)} %get-tuple-element.8), channel_id=1, source_target_pairs={{0,28},{4,24},{8,20},{12,16},{16,12},{20,8},{24,4},{28,0},{1,29},{... | collective-permute-start | bytes 393224 | tf_op jit(solution)/shard_map/cond/branch_0_fun/ppermute | solution.py:711
  148.8 9.6 %collective-permute-done = bf16[4,16384]{1,0:T(4,128)(2,1)S(1)} collective-permute-done((bf16[4,16384]{1,0:T(4,128)(2,1)S(1)}, bf16[4,16384]{1,0:T(4,128)(2,1)S(1)}, u32[]{:S(2)}, u32[]{:S(2)}) %collective-permute-start) | collective-permute-done | bytes 131104 | tf_op jit(solution)/shard_map/cond/branch_0_fun/ppermute | solution.py:711
  158.4 6.9 %collective-permute-start.22 = (bf16[4,16384]{1,0:T(4,128)(2,1)S(1)}, bf16[4,16384]{1,0:T(4,128)(2,1)S(1)}, u32[]{:S(2)}, u32[]{:S(2)}) collective-permute-start(bf16[4,16384]{1,0:T(4,128)(2,1)S(1)} %get-tuple-element.85), channel_id=1, source_target_pairs={{0,12},{4,8},{8,4},{12,0},{16,28},{20,24},{24,20},{28,16},{1,13},{... | collective-permute-start | bytes 393224 | tf_op jit(solution)/shard_map/ppermute | solution.py:711
  166.4 3.3 %collective-permute-done.24 = f32[2,4]{0,1:T(4,128)S(1)} collective-permute-done((f32[2,4]{0,1:T(4,128)S(1)}, f32[2,4]{0,1:T(4,128)S(1)}, u32[]{:S(2)}, u32[]{:S(2)}) %collective-permute-start.24) | collective-permute-done | bytes 64 | tf_op jit(solution)/shard_map/ppermute | solution.py:711
  170.4 3.1 %collective-permute-done.25 = f32[4,4]{0,1:T(4,128)S(1)} collective-permute-done((f32[4,4]{0,1:T(4,128)S(1)}, f32[4,4]{0,1:T(4,128)S(1)}, u32[]{:S(2)}, u32[]{:S(2)}) %collective-permute-start.25) | collective-permute-done | bytes 96 | tf_op jit(solution)/shard_map/ppermute | solution.py:711
  173.6 2.8 %collective-permute-start.26 = (f32[8,4]{0,1:T(4,128)S(1)}, f32[8,4]{0,1:T(4,128)S(1)}, u32[]{:S(2)}, u32[]{:S(2)}) collective-permute-start(f32[8,4]{0,1:T(4,128)S(1)} %pad_maximum_fusion.1), channel_id=1, source_target_pairs={{0,16},{4,20},{8,24},{12,28},{16,0},{20,4},{24,8},{28,12},{1,17},{... | collective-permute-start | bytes 392 | tf_op jit(solution)/shard_map/ppermute | solution.py:711
  (78 shorter events, 26.3 us)
Async XLA Ops:
  9.9 12.4 %collective-permute-start.3 = (bf16[2,2,224,1920]{3,2,1,0:T(8,128)(2,1)}, bf16[2,2,224,1920]{3,2,1,0:T(8,128)(2,1)}, u32[]{:S(2)}, u32[]{:S(2)}) collective-permute-start(bf16[2,2,224,1920]{3,2,1,0:T(8,128)(2,1)} %shard_map.79), channel_id=1, source_target_pairs={{0,1},{1,0},{2,3},{3,2},{4,5},{5,4},{6,7},{7,6},{8,9},{9,8},{10,11... | collective-permute-start | bytes 10321928 | tf_op jit(solution)/shard_map/ppermute | solution.py:711
  15.5 24.3 %collective-permute-start.6 = (bf16[2,2,224,1920]{3,2,1,0:T(8,128)(2,1)}, bf16[2,2,224,1920]{3,2,1,0:T(8,128)(2,1)}, u32[]{:S(2)}, u32[]{:S(2)}) collective-permute-start(bf16[2,2,224,1920]{3,2,1,0:T(8,128)(2,1)} %shard_map.81), channel_id=1, source_target_pairs={{0,1},{1,0},{2,3},{3,2},{4,5},{5,4},{6,7},{7,6},{8,9},{9,8},{10,11... | collective-permute-start | bytes 10321928 | tf_op jit(solution)/shard_map/ppermute | solution.py:711
  36.9 25.4 %collective-permute-start.5 = (bf16[2,2,224,1920]{3,2,1,0:T(8,128)(2,1)}, bf16[2,2,224,1920]{3,2,1,0:T(8,128)(2,1)S(1)}, u32[]{:S(2)}, u32[]{:S(2)}) collective-permute-start(bf16[2,2,224,1920]{3,2,1,0:T(8,128)(2,1)} %get-tuple-element.56), channel_id=1, source_target_pairs={{0,1},{1,0},{2,3},{3,2},{4,5},{5,4},{6,7},{7,6},{8,9},{9,8},{10,11... | collective-permute-start | bytes 10321928 | tf_op jit(solution)/shard_map/ppermute | solution.py:711
  37.4 52.6 %collective-permute-start.4 = (bf16[2,2,224,1920]{3,2,1,0:T(8,128)(2,1)}, bf16[2,2,224,1920]{3,2,1,0:T(8,128)(2,1)S(1)}, u32[]{:S(2)}, u32[]{:S(2)}) collective-permute-start(bf16[2,2,224,1920]{3,2,1,0:T(8,128)(2,1)} %get-tuple-element.55), channel_id=1, source_target_pairs={{0,1},{1,0},{2,3},{3,2},{4,5},{5,4},{6,7},{7,6},{8,9},{9,8},{10,11... | collective-permute-start | bytes 10321928 | tf_op jit(solution)/shard_map/ppermute | solution.py:711
  37.4 23.1 %collective-permute-start.7 = (bf16[1,8,128,128]{3,2,1,0:T(8,128)(2,1)S(1)}, bf16[1,8,128,128]{3,2,1,0:T(8,128)(2,1)S(1)}, u32[]{:S(2)}, u32[]{:S(2)}) collective-permute-start(bf16[1,8,128,128]{3,2,1,0:T(8,128)(2,1)S(1)} %get-tuple-element.62), channel_id=1, source_target_pairs={{0,2},{1,3},{2,0},{3,1},{4,6},{5,7},{6,4},{7,5},{8,10},{9,11},{10,... | collective-permute-start | bytes 786440 | tf_op jit(solution)/shard_map/ppermute | solution.py:711
  60.5 26.1 %collective-permute-start.8 = (bf16[2,8,128,128]{3,2,1,0:T(8,128)(2,1)S(1)}, bf16[2,8,128,128]{3,2,1,0:T(8,128)(2,1)S(1)}, u32[]{:S(2)}, u32[]{:S(2)}) collective-permute-start(bf16[2,8,128,128]{3,2,1,0:T(8,128)(2,1)S(1)} %get-tuple-element.66), channel_id=1, source_target_pairs={{0,2},{1,3},{2,0},{3,1},{4,6},{5,7},{6,4},{7,5},{8,10},{9,11},{10,... | collective-permute-start | bytes 1572872 | tf_op jit(solution)/shard_map/ppermute | solution.py:711
  60.6 25.9 %collective-permute-start.9 = (bf16[1,8,128,128]{3,2,1,0:T(8,128)(2,1)S(1)}, bf16[1,8,128,128]{3,2,1,0:T(8,128)(2,1)S(1)}, u32[]{:S(2)}, u32[]{:S(2)}) collective-permute-start(bf16[1,8,128,128]{3,2,1,0:T(8,128)(2,1)S(1)} %shard_map.83.refs_7_), channel_id=1, source_target_pairs={{0,4},{4,0},{8,12},{12,8},{16,20},{20,16},{24,28},{28,24},{1,5},{5... | collective-permute-start | bytes 786440 | tf_op jit(solution)/shard_map/ppermute | solution.py:711
  85.0 28.1 %collective-permute-start.10 = (bf16[2,8,128,128]{3,2,1,0:T(8,128)(2,1)S(1)}, bf16[2,8,128,128]{3,2,1,0:T(8,128)(2,1)S(1)}, u32[]{:S(2)}, u32[]{:S(2)}) collective-permute-start(bf16[2,8,128,128]{3,2,1,0:T(8,128)(2,1)S(1)} %get-tuple-element.72), channel_id=1, source_target_pairs={{0,2},{1,3},{2,0},{3,1},{4,6},{5,7},{6,4},{7,5},{8,10},{9,11},{10,... | collective-permute-start | bytes 1572872 | tf_op jit(solution)/shard_map/ppermute | solution.py:711
  86.7 26.4 %collective-permute-start.11 = (bf16[1,8,128,128]{3,2,1,0:T(8,128)(2,1)S(1)}, bf16[1,8,128,128]{3,2,1,0:T(8,128)(2,1)S(1)}, u32[]{:S(2)}, u32[]{:S(2)}) collective-permute-start(bf16[1,8,128,128]{3,2,1,0:T(8,128)(2,1)S(1)} %get-tuple-element.68.refs_7_), channel_id=1, source_target_pairs={{0,8},{4,12},{8,0},{12,4},{16,24},{20,28},{24,16},{28,20},{1,9},{5... | collective-permute-start | bytes 786440 | tf_op jit(solution)/shard_map/ppermute | solution.py:711
  88.1 25.0 %collective-permute-start.12 = (bf16[1,8,128,128]{3,2,1,0:T(8,128)(2,1)S(1)}, bf16[1,8,128,128]{3,2,1,0:T(8,128)(2,1)S(1)}, u32[]{:S(2)}, u32[]{:S(2)}) collective-permute-start(bf16[1,8,128,128]{3,2,1,0:T(8,128)(2,1)S(1)} %get-tuple-element.69.refs_8_), channel_id=1, source_target_pairs={{0,4},{4,0},{8,12},{12,8},{16,20},{20,16},{24,28},{28,24},{1,5},{5... | collective-permute-start | bytes 786440 | tf_op jit(solution)/shard_map/ppermute | solution.py:711
  112.5 17.0 %collective-permute-start.15 = (bf16[2,8,128,128]{3,2,1,0:T(8,128)(2,1)S(1)}, bf16[2,8,128,128]{3,2,1,0:T(8,128)(2,1)S(1)}, u32[]{:S(2)}, u32[]{:S(2)}) collective-permute-start(bf16[2,8,128,128]{3,2,1,0:T(8,128)(2,1)S(1)} %get-tuple-element.78), channel_id=1, source_target_pairs={{0,2},{1,3},{2,0},{3,1},{4,6},{5,7},{6,4},{7,5},{8,10},{9,11},{10,... | collective-permute-start | bytes 1572872 | tf_op jit(solution)/shard_map/ppermute | solution.py:711
  113.3 21.1 %collective-permute-start.14 = (bf16[1,8,128,128]{3,2,1,0:T(8,128)(2,1)S(1)}, bf16[1,8,128,128]{3,2,1,0:T(8,128)(2,1)S(1)}, u32[]{:S(2)}, u32[]{:S(2)}) collective-permute-start(bf16[1,8,128,128]{3,2,1,0:T(8,128)(2,1)S(1)} %get-tuple-element.75.refs_4_), channel_id=1, source_target_pairs={{0,16},{4,20},{8,24},{12,28},{16,0},{20,4},{24,8},{28,12},{1,17},{... | collective-permute-start | bytes 786440 | tf_op jit(solution)/shard_map/ppermute | solution.py:711
  114.8 14.7 %collective-permute-start.16 = (bf16[1,8,128,128]{3,2,1,0:T(8,128)(2,1)S(1)}, bf16[1,8,128,128]{3,2,1,0:T(8,128)(2,1)S(1)}, u32[]{:S(2)}, u32[]{:S(2)}) collective-permute-start(bf16[1,8,128,128]{3,2,1,0:T(8,128)(2,1)S(1)} %get-tuple-element.74.refs_3_), channel_id=1, source_target_pairs={{0,4},{4,0},{8,12},{12,8},{16,20},{20,16},{24,28},{28,24},{1,5},{5... | collective-permute-start | bytes 786440 | tf_op jit(solution)/shard_map/ppermute | solution.py:711
  127.9 6.4 %collective-permute-start.13 = (bf16[1,8,128,128]{3,2,1,0:T(8,128)(2,1)S(1)}, bf16[1,8,128,128]{3,2,1,0:T(8,128)(2,1)S(1)}, u32[]{:S(2)}, u32[]{:S(2)}) collective-permute-start(bf16[1,8,128,128]{3,2,1,0:T(8,128)(2,1)S(1)} %get-tuple-element.77), channel_id=1, source_target_pairs={{0,2},{1,3},{2,0},{3,1},{4,6},{5,7},{6,4},{7,5},{8,10},{9,11},{10,... | collective-permute-start | bytes 786440 | tf_op jit(solution)/shard_map/ppermute | solution.py:711
  129.6 6.4 %collective-permute-start.17 = (bf16[1,8,128,128]{3,2,1,0:T(8,128)(2,1)S(1)}, bf16[1,8,128,128]{3,2,1,0:T(8,128)(2,1)S(1)}, u32[]{:S(2)}, u32[]{:S(2)}) collective-permute-start(bf16[1,8,128,128]{3,2,1,0:T(8,128)(2,1)S(1)} %get-tuple-element.79), channel_id=1, source_target_pairs={{0,8},{4,12},{8,0},{12,4},{16,24},{20,28},{24,16},{28,20},{1,9},{5... | collective-permute-start | bytes 786440 | tf_op jit(solution)/shard_map/ppermute | solution.py:711
  129.8 6.4 %collective-permute-start.18 = (bf16[1,8,128,128]{3,2,1,0:T(8,128)(2,1)S(1)}, bf16[1,8,128,128]{3,2,1,0:T(8,128)(2,1)S(1)}, u32[]{:S(2)}, u32[]{:S(2)}) collective-permute-start(bf16[1,8,128,128]{3,2,1,0:T(8,128)(2,1)S(1)} %get-tuple-element.80), channel_id=1, source_target_pairs={{0,4},{4,0},{8,12},{12,8},{16,20},{20,16},{24,28},{28,24},{1,5},{5... | collective-permute-start | bytes 786440 | tf_op jit(solution)/shard_map/ppermute | solution.py:711
  139.2 26.2 %collective-permute-start.20 = (bf16[4,16384]{1,0:T(4,128)(2,1)S(1)}, bf16[4,16384]{1,0:T(4,128)(2,1)S(1)}, u32[]{:S(2)}, u32[]{:S(2)}) collective-permute-start(bf16[4,16384]{1,0:T(4,128)(2,1)S(1)} %get-tuple-element.83), channel_id=1, source_target_pairs={{0,4},{4,0},{8,12},{12,8},{16,20},{20,16},{24,28},{28,24},{1,5},{5... | collective-permute-start | bytes 393224 | tf_op jit(solution)/shard_map/ppermute | solution.py:711
  140.9 35.5 %collective-permute-start.21 = (bf16[4,16384]{1,0:T(4,128)(2,1)S(1)}, bf16[4,16384]{1,0:T(4,128)(2,1)S(1)}, u32[]{:S(2)}, u32[]{:S(2)}) collective-permute-start(bf16[4,16384]{1,0:T(4,128)(2,1)S(1)} %get-tuple-element.84), channel_id=1, source_target_pairs={{0,8},{4,12},{8,0},{12,4},{16,24},{20,28},{24,16},{28,20},{1,9},{5... | collective-permute-start | bytes 393224 | tf_op jit(solution)/shard_map/ppermute | solution.py:711
  142.6 15.8 %collective-permute-start = (bf16[4,16384]{1,0:T(4,128)(2,1)S(1)}, bf16[4,16384]{1,0:T(4,128)(2,1)S(1)}, u32[]{:S(2)}, u32[]{:S(2)}) collective-permute-start(bf16[4,16384]{1,0:T(4,128)(2,1)S(1)} %get-tuple-element.6), channel_id=1, source_target_pairs={{0,20},{4,16},{8,28},{12,24},{16,4},{20,0},{24,12},{28,8},{1,21},{... | collective-permute-start | bytes 393224 | tf_op jit(solution)/shard_map/cond/branch_0_fun/ppermute | solution.py:711
  144.1 14.3 %collective-permute-start.1 = (bf16[4,16384]{1,0:T(4,128)(2,1)S(1)}, bf16[4,16384]{1,0:T(4,128)(2,1)S(1)}, u32[]{:S(2)}, u32[]{:S(2)}) collective-permute-start(bf16[4,16384]{1,0:T(4,128)(2,1)S(1)} %get-tuple-element.7), channel_id=1, source_target_pairs={{0,24},{4,28},{8,16},{12,20},{16,8},{20,12},{24,0},{28,4},{1,25},{... | collective-permute-start | bytes 393224 | tf_op jit(solution)/shard_map/cond/branch_0_fun/ppermute | solution.py:711
  146.5 11.9 %collective-permute-start.2 = (bf16[4,16384]{1,0:T(4,128)(2,1)S(1)}, bf16[4,16384]{1,0:T(4,128)(2,1)S(1)}, u32[]{:S(2)}, u32[]{:S(2)}) collective-permute-start(bf16[4,16384]{1,0:T(4,128)(2,1)S(1)} %get-tuple-element.8), channel_id=1, source_target_pairs={{0,28},{4,24},{8,20},{12,16},{16,12},{20,8},{24,4},{28,0},{1,29},{... | collective-permute-start | bytes 393224 | tf_op jit(solution)/shard_map/cond/branch_0_fun/ppermute | solution.py:711
  158.4 18.0 %collective-permute-start.22 = (bf16[4,16384]{1,0:T(4,128)(2,1)S(1)}, bf16[4,16384]{1,0:T(4,128)(2,1)S(1)}, u32[]{:S(2)}, u32[]{:S(2)}) collective-permute-start(bf16[4,16384]{1,0:T(4,128)(2,1)S(1)} %get-tuple-element.85), channel_id=1, source_target_pairs={{0,12},{4,8},{8,4},{12,0},{16,28},{20,24},{24,20},{28,16},{1,13},{... | collective-permute-start | bytes 393224 | tf_op jit(solution)/shard_map/ppermute | solution.py:711
  165.3 11.0 %collective-permute-start.23 = (bf16[4,16384]{1,0:T(4,128)(2,1)S(1)}, bf16[4,16384]{1,0:T(4,128)(2,1)S(1)}, u32[]{:S(2)}, u32[]{:S(2)}) collective-permute-start(bf16[4,16384]{1,0:T(4,128)(2,1)S(1)} %get-tuple-element.86), channel_id=1, source_target_pairs={{0,16},{4,20},{8,24},{12,28},{16,0},{20,4},{24,8},{28,12},{1,17},{... | collective-permute-start | bytes 393224 | tf_op jit(solution)/shard_map/ppermute | solution.py:711
  173.6 4.5 %collective-permute-start.26 = (f32[8,4]{0,1:T(4,128)S(1)}, f32[8,4]{0,1:T(4,128)S(1)}, u32[]{:S(2)}, u32[]{:S(2)}) collective-permute-start(f32[8,4]{0,1:T(4,128)S(1)} %pad_maximum_fusion.1), channel_id=1, source_target_pairs={{0,16},{4,20},{8,24},{12,28},{16,0},{20,4},{24,8},{28,12},{1,17},{... | collective-permute-start | bytes 392 | tf_op jit(solution)/shard_map/ppermute | solution.py:711
  (10 other events, 71.1 us)

commit v2 on v1

--- a/solution.py
+++ b/solution.py
@@ -13,9 +13,10 @@
 DEPTH = 256
 TOGETHER = 4
 STEP = 3
-LADDER_VMEM = 52 * 1024 * 1024
+LADDER_VMEM = 34 * 1024 * 1024
+FIRST_VMEM = 46 * 1024 * 1024
 SMALL_VMEM = 24 * 1024 * 1024
-GATHER_VMEM = 60 * 1024 * 1024
+GATHER_VMEM = 62 * 1024 * 1024
 HBM = pl.BlockSpec(memory_space=pltpu.HBM)
 
 
@@ -39,9 +40,34 @@
             self.size += size
 
 
+def gather_copies(plan, layout, factors_ref, out_ref, begin, staged, load_sems, store_sems):
+    loads, stores = [], []
+    for t in range(out_ref.shape[0]):
+        for start in (layout.partner_first, layout.partner_second):
+            n = len(loads)
+            source = factors_ref.at[plan[start + begin + t]]
+            loads.append(pltpu.make_async_copy(source, staged.at[n], load_sems.at[n]))
+            stores.append(pltpu.make_async_copy(staged.at[n], out_ref.at[t, n % 2], store_sems.at[n]))
+    return loads, stores
+
+
+def run_gather(loads, stores):
+    for load in loads:
+        load.start()
+    for load, store in zip(loads, stores):
+        load.wait()
+        store.start()
+    for store in stores:
+        store.wait()
+
+
+def over(x, divisor):
+    return lax.shift_right_logical(x * (65536 // divisor + 1), 16)
+
+
 def plan_kernel(
-    place, table, plan, tile_of, home_of, official, wide_of, spot, room, load, used, slot_tile, slot_home, good,
-    *, layout, names, clusters, homes
+    place, table, factors_ref, plan, group_ref, tile_of, home_of, official, wide_of, spot, room, load, used, slot_tile, slot_home, good,
+    staged, load_sems, store_sems, *, layout, names, clusters, homes
 ):
     wide, half = place[0], place[1]
     owners = len(names)
@@ -62,7 +88,7 @@
         return count + (entry & 1)
 
     total = table.shape[0]
-    lax.fori_loop(0, total, list_tile, 0, unroll=5 if total % 5 == 0 else 1)
+    lax.fori_loop(0, total, list_tile, 0, unroll=25 if total % 25 == 0 else 1)
 
     def clear_wide(w):
         room[w] = SLOTS
@@ -78,7 +104,7 @@
         entry = home_of[i] // SLOTS
         official[i] = entry % filled
         home_of[i] = entry // filled
-        wide_of[i] = home_of[i] // homes
+        wide_of[i] = over(home_of[i], homes)
         load[wide_of[i]] = load[wide_of[i]] + 1
         spot[i] = -1
 
@@ -141,6 +167,32 @@
 
             each(across - 1, try_near)
 
+            def try_move(j):
+                at = spot[j]
+                w, h, other = at // SLOTS, wide_of[i], wide_of[j]
+                fits = (at >= 0) & (w != h) & ((w ^ h) < across) & ((w ^ other) < across) & (other != h)
+
+                @pl.when((spot[i] < 0) & fits)
+                def _():
+                    def try_other(k):
+                        to = w ^ (k + 1)
+                        free = (room[to] > 0) & (used[w * owners + h] == 0)
+                        good_place = (to == other) | (used[to * owners + other] == 0)
+
+                        @pl.when((spot[i] < 0) & free & good_place)
+                        def _():
+                            used[w * owners + other] = 0
+                            used[to * owners + other] = 1
+                            put(j, to)
+                            spot[i] = at
+                            used[w * owners + h] = 1
+
+                    each(across - 1, try_other)
+
+            @pl.when(spot[i] < 0)
+            def _():
+                each(filled, try_move)
+
             @pl.when(spot[i] < 0)
             def _():
                 good[0] = 0
@@ -175,11 +227,16 @@
 
     for j, name in enumerate(names):
         base = (wide ^ name) * SLOTS
-        own, other = slot_tile[base + half], slot_tile[base + 1 - half]
-        plan[layout.own_first + j] = own // clusters
-        plan[layout.own_second + j] = own % clusters
-        plan[layout.partner_first + j] = other // clusters
-        plan[layout.partner_second + j] = other % clusters
+        other = slot_tile[base + 1 - half]
+        plan[layout.partner_first + j] = over(other, clusters)
+        plan[layout.partner_second + j] = other - over(other, clusters) * clusters
+    loads, stores = gather_copies(plan, layout, factors_ref, group_ref, 0, staged, load_sems, store_sems)
+    for load in loads:
+        load.start()
+    for j, name in enumerate(names):
+        own = slot_tile[(wide ^ name) * SLOTS + half]
+        plan[layout.own_first + j] = over(own, clusters)
+        plan[layout.own_second + j] = own - over(own, clusters) * clusters
 
     def at_home(slot, w):
         local = slot_home[slot] - w * homes
@@ -202,21 +259,35 @@
     each(owners - 1, meet_later)
     plan[layout.matched] = good[0]
     plan[layout.half] = half
-
-
-def make_plan(place, tile_mask, owner_slot, home_slot, layout, names, clusters, homes):
+    for load, store in zip(loads, stores):
+        load.wait()
+        store.start()
+    for store in stores:
+        store.wait()
+
+
+def make_plan(place, tile_mask, owner_slot, home_slot, factors, layout, names, homes, count):
     owners = len(names)
     filled = owners * SLOTS
     smem = pl.BlockSpec(memory_space=pltpu.SMEM)
     lists = [filled + 1] * 3 + [filled] * 2 + [owners] * 2 + [owners * owners] + [filled] * 2 + [1]
+    clusters, rows, columns = factors.shape
     return pl.pallas_call(
         functools.partial(plan_kernel, layout=layout, names=names, clusters=clusters, homes=homes),
-        in_specs=[smem] * 2,
-        out_specs=smem,
-        out_shape=jax.ShapeDtypeStruct((layout.size,), jnp.int32),
-        scratch_shapes=[pltpu.SMEM((size,), jnp.int32) for size in lists],
-        compiler_params=pltpu.CompilerParams(vmem_limit_bytes=SMALL_VMEM),
-    )(place, tile_mask + SLOTS * (owner_slot + filled * home_slot))
+        in_specs=[smem, smem, HBM],
+        out_specs=[smem, HBM],
+        out_shape=[
+            jax.ShapeDtypeStruct((layout.size,), jnp.int32),
+            jax.ShapeDtypeStruct((count, 2, rows, columns), factors.dtype),
+        ],
+        scratch_shapes=[pltpu.SMEM((size,), jnp.int32) for size in lists]
+        + [
+            pltpu.VMEM((2 * count, rows, columns), factors.dtype),
+            pltpu.SemaphoreType.DMA((2 * count,)),
+            pltpu.SemaphoreType.DMA((2 * count,)),
+        ],
+        compiler_params=pltpu.CompilerParams(vmem_limit_bytes=GATHER_VMEM),
+    )(place, tile_mask + SLOTS * (owner_slot + filled * home_slot), factors)
 
 
 def turn_columns(source, target, slot, d, place):
@@ -237,7 +308,7 @@
     keep_ref, send_ref = take(2)
     handed = [] if is_last else take(2)
     gathered = take(len(gathers))
-    turned_first, turned_second, integral, total, sems = take(5)
+    turned_first, turned_second, integral, total, kron, sems = take(6)
     staged, load_sems, store_sems = take(3) if gathers else (None, None, None)
     turned = (turned_first, turned_second)
     step = pl.program_id(0)
@@ -247,6 +318,7 @@
     blocks = WIDTH // ROWS
     places = (0, DEPTH)
 
+    fill = pltpu.make_async_copy(kron_ref, kron, sems.at[4])
     loads, stores = [], []
     for group, (begin, count) in zip(gathered, gathers):
         for t in range(count):
@@ -267,10 +339,12 @@
                     turned[which][:, :, place + rows : place + DEPTH] = blank
                     for d in range(window):
                         turn_columns(given[2 * which + half], turned[which], 0, d, place)
+            fill.start()
         else:
             takes = [pltpu.make_async_copy(given[i], turned[i].at[0], sems.at[i]) for i in range(2)]
             for copy in takes:
                 copy.start()
+            fill.start()
             if not is_last:
                 blank = jnp.zeros((window * WIDTH, DEPTH - rows), jnp.bfloat16)
                 for which in range(2):
@@ -313,13 +387,17 @@
         def _():
             hand_on(0).start()
 
+    @pl.when(step == 0)
+    def _():
+        fill.wait()
+
     for d in range(0, window, STEP):
         parts = range(d, min(d + STEP, window))
         left = jnp.concatenate(
             [integral[:, e * WIDTH : (e + 1) * WIDTH, :].reshape(blocks * WIDTH, DEPTH) for e in parts], axis=1
         )
         product = jnp.dot(
-            left, kron_ref[d * DEPTH : (d + len(parts)) * DEPTH, :], preferred_element_type=jnp.float32
+            left, kron[d * DEPTH : (d + len(parts)) * DEPTH, :], preferred_element_type=jnp.float32
         )
         if not is_last:
             for e in parts:
@@ -356,7 +434,7 @@
     is_first = given is None
     first, second = layout.own_first + begin, layout.own_second + begin
     operands = [kron]
-    in_specs = [pl.BlockSpec(kron.shape, lambda j, p: (0, 0), pipeline_mode=once)]
+    in_specs = [HBM]
     skip = 1 if is_first else 0
     if not is_last:
         operands += [factors, partner, factors, partner]
@@ -395,7 +473,8 @@
         pltpu.VMEM((2,) + turned_shape, jnp.bfloat16),
         pltpu.VMEM((blocks, columns, DEPTH), jnp.bfloat16),
         pltpu.VMEM((blocks * WIDTH, kron.shape[1]), jnp.float32),
-        pltpu.SemaphoreType.DMA((4,)),
+        pltpu.VMEM(kron.shape, kron.dtype),
+        pltpu.SemaphoreType.DMA((5,)),
     ]
     if gathers:
         sides = 2 * sum(count for _, count in gathers)
@@ -424,7 +503,7 @@
             scratch_shapes=scratch_shapes,
         ),
         out_shape=out_shape,
-        compiler_params=pltpu.CompilerParams(vmem_limit_bytes=LADDER_VMEM),
+        compiler_params=pltpu.CompilerParams(vmem_limit_bytes=FIRST_VMEM if is_first else LADDER_VMEM),
         cost_estimate=pl.CostEstimate(
             flops=flops, bytes_accessed=tiles * 4 * rows * columns * 2 + kron.size * 2, transcendentals=0
         ),
@@ -432,20 +511,7 @@
 
 
 def gather_kernel(plan, factors_ref, out_ref, staged, load_sems, store_sems, *, layout, begin):
-    loads, stores = [], []
-    for t in range(out_ref.shape[0]):
-        for side, start in enumerate((layout.partner_first, layout.partner_second)):
-            n = len(loads)
-            source = factors_ref.at[plan[start + begin + t]]
-            loads.append(pltpu.make_async_copy(source, staged.at[n], load_sems.at[n]))
-            stores.append(pltpu.make_async_copy(staged.at[n], out_ref.at[t, side], store_sems.at[n]))
-    for load in loads:
-        load.start()
-    for load, store in zip(loads, stores):
-        load.wait()
-        store.start()
-    for store in stores:
-        store.wait()
+    run_gather(*gather_copies(plan, layout, factors_ref, out_ref, begin, staged, load_sems, store_sems))
 
 
 def gather(plan, layout, factors, begin, count):
@@ -495,7 +561,7 @@
     )(*[array for group in groups for array, _ in group], after)
 
 
-def prepare_kernel(plan, residual_ref, out_ref, token_ref, held_ref, blank, put_sems, load_sems, *, layout):
+def prepare_kernel(plan, residual_ref, after_ref, out_ref, token_ref, held_ref, blank, put_sems, load_sems, *, layout):
     blank[...] = jnp.zeros_like(blank)
     token_ref[...] = jnp.zeros_like(token_ref)
 
@@ -530,11 +596,11 @@
             load(t).wait()
 
 
-def prepare(plan, layout, residual, tiles):
+def prepare(plan, layout, residual, tiles, after):
     grid_spec = pltpu.PrefetchScalarGridSpec(
         num_scalar_prefetch=1,
         grid=(1,),
-        in_specs=[HBM],
+        in_specs=[HBM, HBM],
         out_specs=[
             HBM,
             pl.BlockSpec((8, WIDTH), lambda i, p: (0, 0)),
@@ -554,12 +620,30 @@
             jax.ShapeDtypeStruct((8, WIDTH), jnp.float32),
             jax.ShapeDtypeStruct((tiles,) + residual.shape[1:], residual.dtype),
         ],
+        compiler_params=pltpu.CompilerParams(vmem_limit_bytes=LADDER_VMEM),
+    )(plan, residual, after)
+
+
+def mark_kernel(plan, out_ref):
+    out_ref[...] = jnp.full(out_ref.shape, plan[0], out_ref.dtype)
+
+
+def mark(plan):
+    return pl.pallas_call(
+        mark_kernel,
+        grid_spec=pltpu.PrefetchScalarGridSpec(
+            num_scalar_prefetch=1,
+            grid=(1,),
+            in_specs=[],
+            out_specs=pl.BlockSpec((8, WIDTH), lambda i, p: (0, 0)),
+        ),
+        out_shape=jax.ShapeDtypeStruct((8, WIDTH), jnp.int32),
         compiler_params=pltpu.CompilerParams(vmem_limit_bytes=GATHER_VMEM),
-    )(plan, residual)
+    )(plan)
 
 
 def finish_kernel(plan, *refs, layout):
-    parts, (keep_ref, send_ref, turned) = refs[:-3], refs[-3:]
+    parts, (keep_ref, send_ref, turned) = refs[:-4], refs[-3:]
     pairs = keep_ref.shape[0]
     half = plan[layout.half]
     mine = half * pairs * ROWS
@@ -576,20 +660,20 @@
                 ref[:, lanes] = piece.astype(jnp.bfloat16)
 
 
-def finish(plan, layout, parts, pairs):
+def finish(plan, layout, parts, pairs, after):
     out = jax.ShapeDtypeStruct((pairs, WIDTH * WIDTH), jnp.bfloat16)
     return pl.pallas_call(
         functools.partial(finish_kernel, layout=layout),
         grid_spec=pltpu.PrefetchScalarGridSpec(
             num_scalar_prefetch=1,
             grid=(1,),
-            in_specs=[pl.BlockSpec(part.shape, lambda i, h: (0, 0, 0, 0)) for part in parts],
+            in_specs=[pl.BlockSpec(part.shape, lambda i, h: (0, 0, 0, 0)) for part in parts] + [HBM],
             out_specs=[pl.BlockSpec(out.shape, lambda i, h: (0, 0))] * 2,
             scratch_shapes=[pltpu.VMEM((WIDTH // ROWS, WIDTH, WIDTH), jnp.float32)],
         ),
         out_shape=[out, out],
         compiler_params=pltpu.CompilerParams(vmem_limit_bytes=SMALL_VMEM),
-    )(plan, *parts)
+    )(plan, *parts, after)
 
 
 def pick_kernel(plan, own_ref, other_ref, *slot_refs, layout):
@@ -732,20 +816,20 @@
     names = sending_order(owner_count)
     layout = Layout(owner_count, home_count)
     place = jnp.stack([wide, half]).astype(jnp.int32)
-    plan = make_plan(place, tile_mask, owner_slot, home_slot, layout, names, factors.shape[0], home_count)
 
     most = max(1, owner_count // 4)
     ends = [1] + list(range(1 + most, owner_count - 1, most)) + [owner_count - 1, owner_count]
     begins = [0] + ends[:-1]
     last = len(ends) - 1
+    plan, group = make_plan(place, tile_mask, owner_slot, home_slot, factors, layout, names, home_count, 2)
     group_ranges = [(0, 2)] + [(begin + 1, end - begin) for begin, end in zip(begins[1:-1], ends[1:-1])]
 
     def exchange_rows(value):
         return exchange(value, "narrow", 1)
 
-    partner_rows = [exchange_rows(gather(plan, layout, factors, *group)) for group in group_ranges[:2]]
+    partner_rows = [exchange_rows(group), exchange_rows(gather(plan, layout, factors, *group_ranges[1]))]
     kron = kron_factor(t2_window, narrow // 2 * (SLOTS * own_pairs))
-    cleared, token, held = prepare(plan, layout, residual_in, owner_count + 1)
+    token = mark(plan)
     arrived = {w: [] for w in range(owner_count)}
     summed = {}
     unsent = [w for w in names if w]
@@ -786,7 +870,8 @@
     while unsent:
         send_wide(last + 1)
 
-    keep, send = finish(plan, layout, list(parts[last]) + arrived[0], own_pairs)
+    cleared, token, held = prepare(plan, layout, residual_in, owner_count + 1, parts[last][0])
+    keep, send = finish(plan, layout, list(parts[last]) + arrived[0], own_pairs, token)
     other = exchange(send, "narrow", 1)
     slots = pick(plan, layout, keep, other, owner_count - 1)
     near = owner_count // 2
@@ -802,8 +887,8 @@
         came += lax.cond(plan[layout.matched] == 1, from_none, from_far, *slots[near:])
 
     norms = mean_squares(plan, layout, keep, other, came[0])[:, :SLOTS].T
-    for bit in range(owner_count.bit_length() - 1):
-        norms = jnp.concatenate([norms, exchange(norms, "wide", 1 << bit)], axis=0)
+    norms = jnp.concatenate([norms] + [exchange(norms, "wide", k) for k in range(1, near)], axis=0)
+    norms = jnp.concatenate([norms, exchange(norms, "wide", near)], axis=0)
     rows = plan[layout.norm : layout.norm + SLOTS]
     here = rows[:, None] == jnp.arange(norms.shape[0], dtype=jnp.int32)[None, :]
     ladder_norms = jnp.sum(jnp.where(here[:, :, None], norms[None], 0.0), axis=1)

time: 179 us -> 140 us (0.78)
  waiting for transfers between devices: 23.7 us -> 8.67 us
  Pallas kernels: 108 us -> 94.7 us
  starting transfers between devices: 35.9 us -> 29.4 us
  local copies, waits for them, and re-layouts: 5.01 us -> 1.21 us
    ppermute x27 -> x25, waiting for transfers between devices: 23.7 us -> 8.67 us  [exchange(): return lax.ppermute(value, axis, [(i, i ^ bit) for i in range(count)])]
    pallas_call x5, Pallas kernels: 88 us -> 75.2 us  [partial_ladders(): pl.pallas_call(functools.partial(partial_kernel, layout=layout, window=wi...]
    ppermute x27 -> x25, starting transfers between devices: 35.9 us -> 29.4 us  [exchange(): return lax.ppermute(value, axis, [(i, i ^ bit) for i in range(count)])]
    unnamed x14 -> x8, local copies, waits for them, and re-layouts: 4.02 us -> 0.02 us
    pallas_call x2 -> x1, Pallas kernels: 7.93 us -> 4.51 us  [gather(): pl.pallas_call(functools.partial(gather_kernel, layout=layout, begin=begi...]
    pallas_call x1, Pallas kernels: 4.34 us -> 6.76 us  [make_plan(): pl.pallas_call(functools.partial(plan_kernel, layout=layout, names=names,...]
  transfers between devices with their start and end apart: 27 -> 25, of which waited for: 8 -> 7; matrix products, arithmetic and copies ran while one was open for 2% -> 2% of each run, Pallas kernels for 55% -> 62%
where the time goes in v2:
time: 140 us; the launch traced here: 139 us
  Pallas kernels  94.7 us (68%)
  starting transfers between devices  29.4 us (21%)
  waiting for transfers between devices  8.67 us (6%)
  other arithmetic  2.74 us (2%)
  between operations  1.56 us (1%)
    pallas_call x5, Pallas kernels, partial_ladders(): pl.pallas_call(functools.partial(partial_kernel, layout=layout, window=wi...  75.2 us
    ppermute x25, starting transfers between devices, exchange(): return lax.ppermute(value, axis, [(i, i ^ bit) for i in range(count)])  29.4 us
    ppermute x25, waiting for transfers between devices, exchange(): return lax.ppermute(value, axis, [(i, i ^ bit) for i in range(count)])  8.67 us
    pallas_call x1, Pallas kernels, make_plan(): pl.pallas_call(functools.partial(plan_kernel, layout=layout, names=names,...  6.76 us
    pallas_call x1, Pallas kernels, gather(): pl.pallas_call(functools.partial(gather_kernel, layout=layout, begin=begi...  4.51 us
  transfers between devices with their start and end apart: 25, of which 7 were waited for; matrix products, arithmetic and copies ran while one was open for 2% of the time, Pallas kernels for 62%

profile of v2, /device:TPU:0, one launch (start us, length us, event | category | flops | bytes accessed | tf_op | source)
XLA Modules:
  0.0 139.5 jit_solution(15849819035566966845)
XLA Ops:
  1.3 1.3 multiply_add_fusion.table
  2.6 6.8 %shard_map.77 = (s32[82]{0:T(128)}, bf16[2,2,224,1920]{3,2,1,0:T(8,128)(2,1)}) custom-call(s32[2]{0:T(128)} %pad_add_fusion.place, s32[225]{0:T(256)} %multiply_add_fusion.table, bf16[15,224,1920]{2,1,0:T(8,128)(2,1)} %refs_3_.7), custom_call_target="tpu_custom_call" | custom-call | tf_op jit(solution)/shard_map/pallas_call | solution.py:275
  9.9 4.5 %shard_map.80 = bf16[2,2,224,1920]{3,2,1,0:T(8,128)(2,1)} custom-call(s32[82]{0:T(128)} %get-tuple-element.54.plan, bf16[15,224,1920]{2,1,0:T(8,128)(2,1)} %refs_3_.7), custom_call_target="tpu_custom_call" | custom-call | tf_op jit(solution)/shard_map/pallas_call | solution.py:519
  14.5 1.2 shard_map.78.refs_9_
  17.3 13.1 %shard_map.79 = (bf16[1,8,128,128]{3,2,1,0:T(8,128)(2,1)S(1)}, bf16[1,8,128,128]{3,2,1,0:T(8,128)(2,1)S(1)}, bf16[1920,512]{1,0:T(8,128)(2,1)S(1)}, bf16[1920,51...) custom-call(s32[82]{0:T(128)S(1)} %copy-done.1, ...), custom_call_target="tpu_custom_call" | custom-call | flops 6039797760 | bytes 5406720 | tf_op jit(solution)/shard_map/pallas_call | solution.py:487
  31.0 2.5 %collective-permute-start.7 = (bf16[1,8,128,128]{3,2,1,0:T(8,128)(2,1)S(1)}, bf16[1,8,128,128]{3,2,1,0:T(8,128)(2,1)S(1)}, u32[]{:S(2)}, u32[]{:S(2)}) collective-permute-start(bf16[1,8,128,128]{3,2,1,0:T(8,128)(2,1)S(1)} %get-tuple-element.63), channel_id=1, source_target_pairs={{0,2},{1,3},{2,0},{3,1},{4,6},{5,7},{6,4},{7,5},{8,10},{9,11},{10,... | collective-permute-start | bytes 786440 | tf_op jit(solution)/shard_map/ppermute | solution.py:795
  33.5 18.3 %shard_map.81 = (bf16[2,8,128,128]{3,2,1,0:T(8,128)(2,1)S(1)}, bf16[2,8,128,128]{3,2,1,0:T(8,128)(2,1)S(1)}, bf16[1920,512]{1,0:T(8,128)(2,1)S(1)}, bf16[1920,512]{1,0:T(8,128)(2,1)S(1)}) custom-call(s32[82]{0:T(128)S(1)} %copy-done.1, bf16[3840,256]{1,0:T(8,128)(2,1)S(1)} %fusion.refs_0_, bf16[15,224,1920]{2,1,0:T(8,128)(2,1)} %refs_3_.7, ...), custom_call_target="tpu_custom_call" | custom-call | flops 12079595520 | bytes 8847360 | tf_op jit(solution)/shard_map/pallas_call | solution.py:487
  52.0 2.5 %collective-permute-start.9 = (bf16[1,8,128,128]{3,2,1,0:T(8,128)(2,1)S(1)}, bf16[1,8,128,128]{3,2,1,0:T(8,128)(2,1)S(1)}, u32[]{:S(2)}, u32[]{:S(2)}) collective-permute-start(bf16[1,8,128,128]{3,2,1,0:T(8,128)(2,1)S(1)} %shard_map.82.refs_7_), channel_id=1, source_target_pairs={{0,4},{4,0},{8,12},{12,8},{16,20},{20,16},{24,28},{28,24},{1,5},{5... | collective-permute-start | bytes 786440 | tf_op jit(solution)/shard_map/ppermute | solution.py:795
  54.5 17.9 %shard_map.83 = (bf16[2,8,128,128]{3,2,1,0:T(8,128)(2,1)S(1)}, bf16[2,8,128,128]{3,2,1,0:T(8,128)(2,1)S(1)}, bf16[1920,512]{1,0:T(8,128)(2,1)S(1)}, bf16[1920,512]{1,0:T(8,128)(2,1)S(1)}) custom-call(s32[82]{0:T(128)S(1)} %copy-done.1, bf16[3840,256]{1,0:T(8,128)(2,1)S(1)} %fusion.refs_0_, bf16[15,224,1920]{2,1,0:T(8,128)(2,1)} %refs_3_.7, ...), custom_call_target="tpu_custom_call" | custom-call | flops 12079595520 | bytes 8847360 | tf_op jit(solution)/shard_map/pallas_call | solution.py:487
  72.6 3.1 %collective-permute-start.11 = (bf16[1,8,128,128]{3,2,1,0:T(8,128)(2,1)S(1)}, bf16[1,8,128,128]{3,2,1,0:T(8,128)(2,1)S(1)}, u32[]{:S(2)}, u32[]{:S(2)}) collective-permute-start(bf16[1,8,128,128]{3,2,1,0:T(8,128)(2,1)S(1)} %get-tuple-element.69.refs_7_), channel_id=1, source_target_pairs={{0,8},{4,12},{8,0},{12,4},{16,24},{20,28},{24,16},{28,20},{1,9},{5... | collective-permute-start | bytes 786440 | tf_op jit(solution)/shard_map/ppermute | solution.py:795
  75.8 1.5 %collective-permute-start.10 = (bf16[2,8,128,128]{3,2,1,0:T(8,128)(2,1)S(1)}, bf16[2,8,128,128]{3,2,1,0:T(8,128)(2,1)S(1)}, u32[]{:S(2)}, u32[]{:S(2)}) collective-permute-start(bf16[2,8,128,128]{3,2,1,0:T(8,128)(2,1)S(1)} %get-tuple-element.73), channel_id=1, source_target_pairs={{0,2},{1,3},{2,0},{3,1},{4,6},{5,7},{6,4},{7,5},{8,10},{9,11},{10,... | collective-permute-start | bytes 1572872 | tf_op jit(solution)/shard_map/ppermute | solution.py:795
  77.3 17.8 %shard_map.85 = (bf16[2,8,128,128]{3,2,1,0:T(8,128)(2,1)S(1)}, bf16[2,8,128,128]{3,2,1,0:T(8,128)(2,1)S(1)}, bf16[1920,512]{1,0:T(8,128)(2,1)S(1)}, bf16[1920,512]{1,0:T(8,128)(2,1)S(1)}) custom-call(s32[82]{0:T(128)S(1)} %copy-done.1, bf16[3840,256]{1,0:T(8,128)(2,1)S(1)} %fusion.refs_0_, bf16[15,224,1920]{2,1,0:T(8,128)(2,1)} %refs_3_.7, ...), custom_call_target="tpu_custom_call" | custom-call | flops 12079595520 | bytes 8847360 | tf_op jit(solution)/shard_map/pallas_call | solution.py:487
  95.8 2.1 %collective-permute-start.16 = (bf16[1,8,128,128]{3,2,1,0:T(8,128)(2,1)S(1)}, bf16[1,8,128,128]{3,2,1,0:T(8,128)(2,1)S(1)}, u32[]{:S(2)}, u32[]{:S(2)}) collective-permute-start(bf16[1,8,128,128]{3,2,1,0:T(8,128)(2,1)S(1)} %get-tuple-element.75.refs_3_), channel_id=1, source_target_pairs={{0,4},{4,0},{8,12},{12,8},{16,20},{20,16},{24,28},{28,24},{1,5},{5... | collective-permute-start | bytes 786440 | tf_op jit(solution)/shard_map/ppermute | solution.py:795
  97.9 1.5 %collective-permute-start.14 = (bf16[1,8,128,128]{3,2,1,0:T(8,128)(2,1)S(1)}, bf16[1,8,128,128]{3,2,1,0:T(8,128)(2,1)S(1)}, u32[]{:S(2)}, u32[]{:S(2)}) collective-permute-start(bf16[1,8,128,128]{3,2,1,0:T(8,128)(2,1)S(1)} %get-tuple-element.76.refs_4_), channel_id=1, source_target_pairs={{0,16},{4,20},{8,24},{12,28},{16,0},{20,4},{24,8},{28,12},{1,17},{... | collective-permute-start | bytes 786440 | tf_op jit(solution)/shard_map/ppermute | solution.py:795
  99.5 8.1 %shard_map.87 = (bf16[1,8,128,128]{3,2,1,0:T(8,128)(2,1)S(1)}, bf16[1,8,128,128]{3,2,1,0:T(8,128)(2,1)S(1)}) custom-call(s32[82]{0:T(128)S(1)} %copy-done.1, bf16[3840,256]{1,0:T(8,128)(2,1)S(1)} %fusion.refs_0_, bf16[1920,512]{1,0:T(8,128)(2,1)S(1)} %get-tuple-element.71.refs_1_, bf16[1920,512]{1,0:T(8,128)(2,1)S(1)} %get-tuple-element.72.refs_2_, ...), custom_call_target="tpu_custom_call" | custom-call | flops 6039797760 | bytes 5406720 | tf_op jit(solution)/shard_map/pallas_call | solution.py:487
  107.6 1.5 %collective-permute-start.13 = (bf16[1,8,128,128]{3,2,1,0:T(8,128)(2,1)S(1)}, bf16[1,8,128,128]{3,2,1,0:T(8,128)(2,1)S(1)}, u32[]{:S(2)}, u32[]{:S(2)}) collective-permute-start(bf16[1,8,128,128]{3,2,1,0:T(8,128)(2,1)S(1)} %get-tuple-element.80), channel_id=1, source_target_pairs={{0,2},{1,3},{2,0},{3,1},{4,6},{5,7},{6,4},{7,5},{8,10},{9,11},{10,... | collective-permute-start | bytes 786440 | tf_op jit(solution)/shard_map/ppermute | solution.py:795
  111.0 2.7 %shard_map.88 = (bf16[29,4,16384]{2,1,0:T(4,128)(2,1)}, f32[8,128]{1,0:T(8,128)S(1)}, bf16[9,4,16384]{2,1,0:T(4,128)(2,1)S(1)}) custom-call(s32[82]{0:T(128)S(1)} %copy-done.1, bf16[29,4,16384]{2,1,0:T(4,128)(2,1)S(1)} %copy-done, bf16[1,8,128,128]{3,2,1,0:T(8,128)(2,1)S(1)} %get-tuple-element.77.after_ref.refs_5_.refs_0_), custom_call_target="tpu_custom_call" | custom-call | tf_op jit(solution)/shard_map/pallas_call | solution.py:615
  114.0 1.8 %collective-permute-done.17.refs_3_ = bf16[1,8,128,128]{3,2,1,0:T(8,128)(2,1)S(1)} collective-permute-done((bf16[1,8,128,128]{3,2,1,0:T(8,128)(2,1)S(1)}, bf16[1,8,128,128]{3,2,1,0:T(8,128)(2,1)S(1)}, u32[]{:S(2)}, u32[]{:S(2)}) %collective-permute-start.17) | collective-permute-done | bytes 262176 | tf_op jit(solution)/shard_map/ppermute | solution.py:795
  120.5 1.9 %collective-permute-start.21 = (bf16[4,16384]{1,0:T(4,128)(2,1)S(1)}, bf16[4,16384]{1,0:T(4,128)(2,1)S(1)}, u32[]{:S(2)}, u32[]{:S(2)}) collective-permute-start(bf16[4,16384]{1,0:T(4,128)(2,1)S(1)} %get-tuple-element.88), channel_id=1, source_target_pairs={{0,8},{4,12},{8,0},{12,4},{16,24},{20,28},{24,16},{28,20},{1,9},{5... | collective-permute-start | bytes 393224 | tf_op jit(solution)/shard_map/ppermute | solution.py:795
  127.1 1.9 %collective-permute-start.25 = (f32[2,4]{0,1:T(4,128)S(1)}, f32[2,4]{0,1:T(4,128)S(1)}, u32[]{:S(2)}, u32[]{:S(2)}) collective-permute-start(f32[2,4]{0,1:T(4,128)S(1)} %slice_bitcast_fusion), channel_id=1, source_target_pairs={{0,8},{4,12},{8,0},{12,4},{16,24},{20,28},{24,16},{28,20},{1,9},{5... | collective-permute-start | bytes 104 | tf_op jit(solution)/shard_map/ppermute | solution.py:795
  129.7 2.4 %collective-permute-start.26 = (f32[2,4]{0,1:T(4,128)S(1)}, f32[2,4]{0,1:T(4,128)S(1)}, u32[]{:S(2)}, u32[]{:S(2)}) collective-permute-start(f32[2,4]{0,1:T(4,128)S(1)} %slice_bitcast_fusion), channel_id=1, source_target_pairs={{0,12},{4,8},{8,4},{12,0},{16,28},{20,24},{24,20},{28,16},{1,13},{... | collective-permute-start | bytes 104 | tf_op jit(solution)/shard_map/ppermute | solution.py:795
  132.1 2.1 %collective-permute-done.26 = f32[2,4]{0,1:T(4,128)S(1)} collective-permute-done((f32[2,4]{0,1:T(4,128)S(1)}, f32[2,4]{0,1:T(4,128)S(1)}, u32[]{:S(2)}, u32[]{:S(2)}) %collective-permute-start.26) | collective-permute-done | bytes 64 | tf_op jit(solution)/shard_map/ppermute | solution.py:795
  135.3 1.4 %shard_map.92 = bf16[29,4,16384]{2,1,0:T(4,128)(2,1)} custom-call(s32[82]{0:T(128)S(1)} %copy-done.1, bf16[29,4,16384]{2,1,0:T(4,128)(2,1)} %get-tuple-element.78.cleared_ref, bf16[9,4,16384]{2,1,0:T(4,128)(2,1)S(1)} %get-tuple-element.79.held_ref, bf16[4,16384]{1,0:T(4,128)(2,1)S(1)} %get-tuple-element.85.own_ref.refs_0_, ...), custom_call_target="tpu_custom_call", output_to_operand_aliasing={{}: (1, {})} | custom-call | tf_op jit(solution)/shard_map/pallas_call | solution.py:768
  136.7 2.0 %collective-permute-done.27 = f32[8,4]{0,1:T(4,128)S(1)} collective-permute-done((f32[8,4]{0,1:T(4,128)S(1)}, f32[8,4]{0,1:T(4,128)S(1)}, u32[]{:S(2)}, u32[]{:S(2)}) %collective-permute-start.27) | collective-permute-done | bytes 160 | tf_op jit(solution)/shard_map/ppermute | solution.py:795
  (70 shorter events, 18.0 us)
Async XLA Ops:
  9.3 8.0 %collective-permute-start.3 = (bf16[2,2,224,1920]{3,2,1,0:T(8,128)(2,1)}, bf16[2,2,224,1920]{3,2,1,0:T(8,128)(2,1)}, u32[]{:S(2)}, u32[]{:S(2)}) collective-permute-start(bf16[2,2,224,1920]{3,2,1,0:T(8,128)(2,1)} %get-tuple-element.55), channel_id=1, source_target_pairs={{0,1},{1,0},{2,3},{3,2},{4,5},{5,4},{6,7},{7,6},{8,9},{9,8},{10,11... | collective-permute-start | bytes 10321928 | tf_op jit(solution)/shard_map/ppermute | solution.py:795
  14.4 19.1 %collective-permute-start.6 = (bf16[2,2,224,1920]{3,2,1,0:T(8,128)(2,1)}, bf16[2,2,224,1920]{3,2,1,0:T(8,128)(2,1)}, u32[]{:S(2)}, u32[]{:S(2)}) collective-permute-start(bf16[2,2,224,1920]{3,2,1,0:T(8,128)(2,1)} %shard_map.80), channel_id=1, source_target_pairs={{0,1},{1,0},{2,3},{3,2},{4,5},{5,4},{6,7},{7,6},{8,9},{9,8},{10,11... | collective-permute-start | bytes 10321928 | tf_op jit(solution)/shard_map/ppermute | solution.py:795
  30.4 24.1 %collective-permute-start.5 = (bf16[2,2,224,1920]{3,2,1,0:T(8,128)(2,1)}, bf16[2,2,224,1920]{3,2,1,0:T(8,128)(2,1)S(1)}, u32[]{:S(2)}, u32[]{:S(2)}) collective-permute-start(bf16[2,2,224,1920]{3,2,1,0:T(8,128)(2,1)} %get-tuple-element.57), channel_id=1, source_target_pairs={{0,1},{1,0},{2,3},{3,2},{4,5},{5,4},{6,7},{7,6},{8,9},{9,8},{10,11... | collective-permute-start | bytes 10321928 | tf_op jit(solution)/shard_map/ppermute | solution.py:795
  30.9 46.3 %collective-permute-start.4 = (bf16[2,2,224,1920]{3,2,1,0:T(8,128)(2,1)}, bf16[2,2,224,1920]{3,2,1,0:T(8,128)(2,1)S(1)}, u32[]{:S(2)}, u32[]{:S(2)}) collective-permute-start(bf16[2,2,224,1920]{3,2,1,0:T(8,128)(2,1)} %get-tuple-element.56), channel_id=1, source_target_pairs={{0,1},{1,0},{2,3},{3,2},{4,5},{5,4},{6,7},{7,6},{8,9},{9,8},{10,11... | collective-permute-start | bytes 10321928 | tf_op jit(solution)/shard_map/ppermute | solution.py:795
  31.0 20.9 %collective-permute-start.7 = (bf16[1,8,128,128]{3,2,1,0:T(8,128)(2,1)S(1)}, bf16[1,8,128,128]{3,2,1,0:T(8,128)(2,1)S(1)}, u32[]{:S(2)}, u32[]{:S(2)}) collective-permute-start(bf16[1,8,128,128]{3,2,1,0:T(8,128)(2,1)S(1)} %get-tuple-element.63), channel_id=1, source_target_pairs={{0,2},{1,3},{2,0},{3,1},{4,6},{5,7},{6,4},{7,5},{8,10},{9,11},{10,... | collective-permute-start | bytes 786440 | tf_op jit(solution)/shard_map/ppermute | solution.py:795
  51.8 20.6 %collective-permute-start.8 = (bf16[2,8,128,128]{3,2,1,0:T(8,128)(2,1)S(1)}, bf16[2,8,128,128]{3,2,1,0:T(8,128)(2,1)S(1)}, u32[]{:S(2)}, u32[]{:S(2)}) collective-permute-start(bf16[2,8,128,128]{3,2,1,0:T(8,128)(2,1)S(1)} %get-tuple-element.67), channel_id=1, source_target_pairs={{0,2},{1,3},{2,0},{3,1},{4,6},{5,7},{6,4},{7,5},{8,10},{9,11},{10,... | collective-permute-start | bytes 1572872 | tf_op jit(solution)/shard_map/ppermute | solution.py:795
  52.0 20.5 %collective-permute-start.9 = (bf16[1,8,128,128]{3,2,1,0:T(8,128)(2,1)S(1)}, bf16[1,8,128,128]{3,2,1,0:T(8,128)(2,1)S(1)}, u32[]{:S(2)}, u32[]{:S(2)}) collective-permute-start(bf16[1,8,128,128]{3,2,1,0:T(8,128)(2,1)S(1)} %shard_map.82.refs_7_), channel_id=1, source_target_pairs={{0,4},{4,0},{8,12},{12,8},{16,20},{20,16},{24,28},{28,24},{1,5},{5... | collective-permute-start | bytes 786440 | tf_op jit(solution)/shard_map/ppermute | solution.py:795
  72.6 23.0 %collective-permute-start.11 = (bf16[1,8,128,128]{3,2,1,0:T(8,128)(2,1)S(1)}, bf16[1,8,128,128]{3,2,1,0:T(8,128)(2,1)S(1)}, u32[]{:S(2)}, u32[]{:S(2)}) collective-permute-start(bf16[1,8,128,128]{3,2,1,0:T(8,128)(2,1)S(1)} %get-tuple-element.69.refs_7_), channel_id=1, source_target_pairs={{0,8},{4,12},{8,0},{12,4},{16,24},{20,28},{24,16},{28,20},{1,9},{5... | collective-permute-start | bytes 786440 | tf_op jit(solution)/shard_map/ppermute | solution.py:795
  75.8 19.9 %collective-permute-start.12 = (bf16[1,8,128,128]{3,2,1,0:T(8,128)(2,1)S(1)}, bf16[1,8,128,128]{3,2,1,0:T(8,128)(2,1)S(1)}, u32[]{:S(2)}, u32[]{:S(2)}) collective-permute-start(bf16[1,8,128,128]{3,2,1,0:T(8,128)(2,1)S(1)} %get-tuple-element.70.refs_8_), channel_id=1, source_target_pairs={{0,4},{4,0},{8,12},{12,8},{16,20},{20,16},{24,28},{28,24},{1,5},{5... | collective-permute-start | bytes 786440 | tf_op jit(solution)/shard_map/ppermute | solution.py:795
  75.8 19.9 %collective-permute-start.10 = (bf16[2,8,128,128]{3,2,1,0:T(8,128)(2,1)S(1)}, bf16[2,8,128,128]{3,2,1,0:T(8,128)(2,1)S(1)}, u32[]{:S(2)}, u32[]{:S(2)}) collective-permute-start(bf16[2,8,128,128]{3,2,1,0:T(8,128)(2,1)S(1)} %get-tuple-element.73), channel_id=1, source_target_pairs={{0,2},{1,3},{2,0},{3,1},{4,6},{5,7},{6,4},{7,5},{8,10},{9,11},{10,... | collective-permute-start | bytes 1572872 | tf_op jit(solution)/shard_map/ppermute | solution.py:795
  95.0 14.1 %collective-permute-start.15 = (bf16[2,8,128,128]{3,2,1,0:T(8,128)(2,1)S(1)}, bf16[2,8,128,128]{3,2,1,0:T(8,128)(2,1)S(1)}, u32[]{:S(2)}, u32[]{:S(2)}) collective-permute-start(bf16[2,8,128,128]{3,2,1,0:T(8,128)(2,1)S(1)} %get-tuple-element.81), channel_id=1, source_target_pairs={{0,2},{1,3},{2,0},{3,1},{4,6},{5,7},{6,4},{7,5},{8,10},{9,11},{10,... | collective-permute-start | bytes 1572872 | tf_op jit(solution)/shard_map/ppermute | solution.py:795
  95.8 13.3 %collective-permute-start.16 = (bf16[1,8,128,128]{3,2,1,0:T(8,128)(2,1)S(1)}, bf16[1,8,128,128]{3,2,1,0:T(8,128)(2,1)S(1)}, u32[]{:S(2)}, u32[]{:S(2)}) collective-permute-start(bf16[1,8,128,128]{3,2,1,0:T(8,128)(2,1)S(1)} %get-tuple-element.75.refs_3_), channel_id=1, source_target_pairs={{0,4},{4,0},{8,12},{12,8},{16,20},{20,16},{24,28},{28,24},{1,5},{5... | collective-permute-start | bytes 786440 | tf_op jit(solution)/shard_map/ppermute | solution.py:795
  97.9 16.1 %collective-permute-start.14 = (bf16[1,8,128,128]{3,2,1,0:T(8,128)(2,1)S(1)}, bf16[1,8,128,128]{3,2,1,0:T(8,128)(2,1)S(1)}, u32[]{:S(2)}, u32[]{:S(2)}) collective-permute-start(bf16[1,8,128,128]{3,2,1,0:T(8,128)(2,1)S(1)} %get-tuple-element.76.refs_4_), channel_id=1, source_target_pairs={{0,16},{4,20},{8,24},{12,28},{16,0},{20,4},{24,8},{28,12},{1,17},{... | collective-permute-start | bytes 786440 | tf_op jit(solution)/shard_map/ppermute | solution.py:795
  107.6 6.4 %collective-permute-start.13 = (bf16[1,8,128,128]{3,2,1,0:T(8,128)(2,1)S(1)}, bf16[1,8,128,128]{3,2,1,0:T(8,128)(2,1)S(1)}, u32[]{:S(2)}, u32[]{:S(2)}) collective-permute-start(bf16[1,8,128,128]{3,2,1,0:T(8,128)(2,1)S(1)} %get-tuple-element.80), channel_id=1, source_target_pairs={{0,2},{1,3},{2,0},{3,1},{4,6},{5,7},{6,4},{7,5},{8,10},{9,11},{10,... | collective-permute-start | bytes 786440 | tf_op jit(solution)/shard_map/ppermute | solution.py:795
  109.3 6.5 %collective-permute-start.17 = (bf16[1,8,128,128]{3,2,1,0:T(8,128)(2,1)S(1)}, bf16[1,8,128,128]{3,2,1,0:T(8,128)(2,1)S(1)}, u32[]{:S(2)}, u32[]{:S(2)}) collective-permute-start(bf16[1,8,128,128]{3,2,1,0:T(8,128)(2,1)S(1)} %get-tuple-element.82), channel_id=1, source_target_pairs={{0,8},{4,12},{8,0},{12,4},{16,24},{20,28},{24,16},{28,20},{1,9},{5... | collective-permute-start | bytes 786440 | tf_op jit(solution)/shard_map/ppermute | solution.py:795
  109.9 6.4 %collective-permute-start.18 = (bf16[1,8,128,128]{3,2,1,0:T(8,128)(2,1)S(1)}, bf16[1,8,128,128]{3,2,1,0:T(8,128)(2,1)S(1)}, u32[]{:S(2)}, u32[]{:S(2)}) collective-permute-start(bf16[1,8,128,128]{3,2,1,0:T(8,128)(2,1)S(1)} %get-tuple-element.83), channel_id=1, source_target_pairs={{0,4},{4,0},{8,12},{12,8},{16,20},{20,16},{24,28},{28,24},{1,5},{5... | collective-permute-start | bytes 786440 | tf_op jit(solution)/shard_map/ppermute | solution.py:795
  119.3 5.9 %collective-permute-start.20 = (bf16[4,16384]{1,0:T(4,128)(2,1)S(1)}, bf16[4,16384]{1,0:T(4,128)(2,1)S(1)}, u32[]{:S(2)}, u32[]{:S(2)}) collective-permute-start(bf16[4,16384]{1,0:T(4,128)(2,1)S(1)} %get-tuple-element.87), channel_id=1, source_target_pairs={{0,4},{4,0},{8,12},{12,8},{16,20},{20,16},{24,28},{28,24},{1,5},{5... | collective-permute-start | bytes 393224 | tf_op jit(solution)/shard_map/ppermute | solution.py:795
  120.5 14.8 %collective-permute-start.21 = (bf16[4,16384]{1,0:T(4,128)(2,1)S(1)}, bf16[4,16384]{1,0:T(4,128)(2,1)S(1)}, u32[]{:S(2)}, u32[]{:S(2)}) collective-permute-start(bf16[4,16384]{1,0:T(4,128)(2,1)S(1)} %get-tuple-element.88), channel_id=1, source_target_pairs={{0,8},{4,12},{8,0},{12,4},{16,24},{20,28},{24,16},{28,20},{1,9},{5... | collective-permute-start | bytes 393224 | tf_op jit(solution)/shard_map/ppermute | solution.py:795
  122.6 12.7 %collective-permute-start.22 = (bf16[4,16384]{1,0:T(4,128)(2,1)S(1)}, bf16[4,16384]{1,0:T(4,128)(2,1)S(1)}, u32[]{:S(2)}, u32[]{:S(2)}) collective-permute-start(bf16[4,16384]{1,0:T(4,128)(2,1)S(1)} %get-tuple-element.89), channel_id=1, source_target_pairs={{0,12},{4,8},{8,4},{12,0},{16,28},{20,24},{24,20},{28,16},{1,13},{... | collective-permute-start | bytes 393224 | tf_op jit(solution)/shard_map/ppermute | solution.py:795
  123.2 12.1 %collective-permute-start.23 = (bf16[4,16384]{1,0:T(4,128)(2,1)S(1)}, bf16[4,16384]{1,0:T(4,128)(2,1)S(1)}, u32[]{:S(2)}, u32[]{:S(2)}) collective-permute-start(bf16[4,16384]{1,0:T(4,128)(2,1)S(1)} %get-tuple-element.90), channel_id=1, source_target_pairs={{0,16},{4,20},{8,24},{12,28},{16,0},{20,4},{24,8},{28,12},{1,17},{... | collective-permute-start | bytes 393224 | tf_op jit(solution)/shard_map/ppermute | solution.py:795
  126.1 3.6 %collective-permute-start.24 = (f32[2,4]{0,1:T(4,128)S(1)}, f32[2,4]{0,1:T(4,128)S(1)}, u32[]{:S(2)}, u32[]{:S(2)}) collective-permute-start(f32[2,4]{0,1:T(4,128)S(1)} %slice_bitcast_fusion), channel_id=1, source_target_pairs={{0,4},{4,0},{8,12},{12,8},{16,20},{20,16},{24,28},{28,24},{1,5},{5... | collective-permute-start | bytes 104 | tf_op jit(solution)/shard_map/ppermute | solution.py:795
  127.1 5.0 %collective-permute-start.25 = (f32[2,4]{0,1:T(4,128)S(1)}, f32[2,4]{0,1:T(4,128)S(1)}, u32[]{:S(2)}, u32[]{:S(2)}) collective-permute-start(f32[2,4]{0,1:T(4,128)S(1)} %slice_bitcast_fusion), channel_id=1, source_target_pairs={{0,8},{4,12},{8,0},{12,4},{16,24},{20,28},{24,16},{28,20},{1,9},{5... | collective-permute-start | bytes 104 | tf_op jit(solution)/shard_map/ppermute | solution.py:795
  129.7 4.5 %collective-permute-start.26 = (f32[2,4]{0,1:T(4,128)S(1)}, f32[2,4]{0,1:T(4,128)S(1)}, u32[]{:S(2)}, u32[]{:S(2)}) collective-permute-start(f32[2,4]{0,1:T(4,128)S(1)} %slice_bitcast_fusion), channel_id=1, source_target_pairs={{0,12},{4,8},{8,4},{12,0},{16,28},{20,24},{24,20},{28,16},{1,13},{... | collective-permute-start | bytes 104 | tf_op jit(solution)/shard_map/ppermute | solution.py:795
  134.2 4.5 %collective-permute-start.27 = (f32[8,4]{0,1:T(4,128)S(1)}, f32[8,4]{0,1:T(4,128)S(1)}, u32[]{:S(2)}, u32[]{:S(2)}) collective-permute-start(f32[8,4]{0,1:T(4,128)S(1)} %pad_maximum_fusion), channel_id=1, source_target_pairs={{0,16},{4,20},{8,24},{12,28},{16,0},{20,4},{24,8},{28,12},{1,17},{... | collective-permute-start | bytes 392 | tf_op jit(solution)/shard_map/ppermute | solution.py:795
  (5 other events, 23.3 us)
